TPU v7x, 512 devices: a whole 4x4x16 slice. The times are simulated.
512 devices in a mesh: grid: 32 (over x_lo, z), member: 16 (over x_hi, y, core).
Axes of the slice: x: 4 (x_hi: 2, x_lo: 2; x = x_hi * 2 + x_lo), y: 4, z: 16, core: 2. Of those that a mesh axis runs over, the one named last changes fastest.
Arguments:
- prior_sample_matrix: bfloat16 [512, 512, 1024], P('member', 'grid'), may hold values from -6 to 6
- cell_class: int32 [512, 1024], P('grid'), may hold values from 0 to 15
- diffusion_table: float32 [16], replicated, may hold values from 0.04 to 0.2
- velocity_table: float32 [2, 16], replicated, may hold values from -0.08 to 0.08
- obs_cells: int32 [32, 32, 128], P('grid'), may hold values from 0 to 16383
- obs_count: int32 [32, 32], P('grid'), may hold values from 16 to 128, as said below
- obs_value: float32 [32, 32, 128], P('grid'), may hold values from -6 to 6
- obs_scale: float32 [32, 32, 128], P('grid'), may hold values from 1 to 3
Outputs:
- predicted_samples: bfloat16 [512, 512, 1024], P('member', 'grid')
- posterior_mean_vector: float32 [512, 1024], P('grid')
- posterior_measured_mean: float32 [32, 32, 128], P('grid')
- mixing_factors: float32 [512], replicated
Inputs may be any that keep to these rules, and one draw needn't show every extreme that they name: Slots at or beyond obs_count are unused; some owner has all 128 slots used from every source rank.
All inputs are finite; a program needn't handle non-finite values.
Results may differ from a plain program's by a relative error of at most 0.011.
Values may be sent and summed in bfloat16 or wider, within the bound.
A program may use at most 64 MiB of HBM per device.

v0:
```python
import jax
import jax.numpy as jnp
from jax import lax
from jax.sharding import PartitionSpec as P

STEPS = 6


HIGH = lax.Precision.HIGHEST


def padded_2(cells, sides, width):
    for axis, dim in sides:
        count = lax.axis_size(axis)
        ends = count - 1
        head = lax.slice_in_dim(cells, 0, width, axis=dim)
        tail = lax.slice_in_dim(cells, cells.shape[dim] - width, cells.shape[dim], axis=dim)
        cells = jnp.concatenate(
            [
                lax.ppermute(tail, axis, [(i, (i + 1) % count) for i in range(ends)]),
                cells,
                lax.ppermute(head, axis, [((i + 1) % count, i) for i in range(ends)]),
            ],
            axis=dim,
        )
    return cells


def shifted(value, axis, steps):
    count = lax.axis_size(axis)
    pairs = [(source, (source + steps) % count) for source in range(count)]
    return lax.ppermute(value, axis, pairs)


def advance(center, above_row, below_row, diffuse, drift_x, drift_y):
    lead = [(0, 0)] * (center.ndim - 1)
    left_col = jnp.pad(center, lead + [(1, 0)])[..., :-1]
    right_col = jnp.pad(center, lead + [(0, 1)])[..., 1:]
    result = (1.0 - 4.0 * diffuse) * center
    result = result + (diffuse + 0.5 * drift_y) * above_row + (diffuse - 0.5 * drift_y) * below_row
    return result + (diffuse + 0.5 * drift_x) * left_col + (diffuse - 0.5 * drift_x) * right_col


def lookup(classes, diffusion_table, velocity_table):
    class_count = diffusion_table.shape[0]
    onehot = (classes[None] == jnp.arange(class_count, dtype=jnp.int32)[:, None, None]).astype(
        jnp.float32
    )
    coef_table = jnp.concatenate([diffusion_table[None], velocity_table], 0)
    cell_coefs = jnp.einsum("kc,crn->krn", coef_table, onehot, precision=HIGH)
    return (cell_coefs[0], cell_coefs[1], cell_coefs[2])


def solve_weights(gram_matrix, right_side):
    sample_count = gram_matrix.shape[0]
    system = gram_matrix + (sample_count - 1) * jnp.eye(sample_count, dtype=gram_matrix.dtype)
    factor = jnp.linalg.cholesky(system)
    column = right_side[:, None]
    inner = lax.linalg.triangular_solve(factor, column, left_side=True, lower=True)
    outer = lax.linalg.triangular_solve(factor, inner, left_side=True, lower=True, transpose_a=True)
    return outer[:, 0]


def local(
    prior_sample_matrix,
    cell_class,
    diffusion_table,
    velocity_table,
    obs_cells,
    obs_count,
    obs_value,
    obs_scale,
):
    subdomain_samples = prior_sample_matrix.shape[0]
    ocean_vector = prior_sample_matrix.astype(jnp.float32)
    diffuse, drift_x, drift_y = lookup(cell_class, diffusion_table, velocity_table)
    for repeat in range(STEPS):
        padded = padded_2(ocean_vector, (("grid", 1),), 1)
        ocean_vector = advance(
            ocean_vector, padded[:, :-2], padded[:, 2:], diffuse, drift_x, drift_y
        )
    predicted_samples = ocean_vector.astype(jnp.bfloat16)
    owners = obs_cells.shape[1]
    slot_cap = obs_cells.shape[2]
    slot_total = owners * slot_cap
    raveled_vector = predicted_samples.reshape(subdomain_samples, -1)
    cell_list = obs_cells[0].reshape(-1)
    picked = jnp.take(raveled_vector, cell_list, axis=1).reshape(
        subdomain_samples, owners, slot_cap
    )
    received = lax.all_to_all(picked, "grid", split_axis=1, concat_axis=1, tiled=True)
    sampled = received.reshape(subdomain_samples, slot_total)
    slot_index = jnp.arange(slot_cap, dtype=jnp.int32)
    valid_slot = (slot_index[None, :] < obs_count[0][:, None]).astype(jnp.float32).reshape(-1)
    weight = obs_scale[0].reshape(-1) * valid_slot
    observed = obs_value[0].reshape(-1)
    cycle_size = lax.axis_size("member")
    member_pos = lax.axis_index("member")
    sample_count = subdomain_samples * cycle_size
    contract = (((1,), (1,)), ((), ()))
    sampled_float = sampled.astype(jnp.float32)
    obs_mean = lax.psum(jnp.sum(sampled_float, axis=0), "member") / sample_count
    anomaly = sampled_float - obs_mean
    panel = (anomaly * weight).astype(jnp.bfloat16)
    departure = (observed - obs_mean) * weight
    right_rows = jnp.dot(panel.astype(jnp.float32), departure, precision=HIGH)

    def place_block(row_block, visitor, offset):
        source = (member_pos - offset) % cycle_size
        gram_block = lax.dot_general(panel, visitor, contract, preferred_element_type=jnp.float32)
        return lax.dynamic_update_slice(row_block, gram_block, (0, source * subdomain_samples))

    row_block = place_block(jnp.zeros((subdomain_samples, sample_count), jnp.float32), panel, 0)

    def cycle_turn(offset, carry):
        visitor, row_block = carry
        visitor = shifted(visitor, "member", 1)
        return (visitor, place_block(row_block, visitor, offset))

    discarded_output, row_block = lax.fori_loop(1, cycle_size, cycle_turn, (panel, row_block))
    row_block, right_rows = lax.psum((row_block, right_rows), "grid")
    gram_matrix, right_side = (
        lax.all_gather(row_block, "member", axis=0, tiled=True),
        lax.all_gather(right_rows, "member", axis=0, tiled=True),
    )
    mixing_factors = solve_weights(gram_matrix, right_side)
    local_weights = lax.dynamic_slice_in_dim(
        mixing_factors, member_pos * subdomain_samples, subdomain_samples
    )
    slot_term = jnp.dot(local_weights, anomaly, precision=HIGH)
    sample_diffusivity = 1.0 / sample_count + mixing_factors - jnp.mean(mixing_factors)
    regional_diffusivity = lax.dynamic_slice_in_dim(
        sample_diffusivity, member_pos * subdomain_samples, subdomain_samples
    )
    field_contribution = jnp.sum(
        regional_diffusivity[:, None, None] * predicted_samples.astype(jnp.float32), axis=0
    )
    posterior_mean_vector, slot_sum = lax.psum((field_contribution, slot_term), "member")
    posterior_measured_mean = (obs_mean + slot_sum).reshape(1, owners, slot_cap)
    return (predicted_samples, posterior_mean_vector, posterior_measured_mean, mixing_factors)


def solution(mesh):
    in_specs = (
        P("member", "grid", None),
        P("grid", None),
        P(),
        P(),
        P("grid", None, None),
        P("grid", None),
        P("grid", None, None),
        P("grid", None, None),
    )
    out_specs = (P("member", "grid", None), P("grid", None), P("grid", None, None), P())
    return jax.shard_map(local, mesh=mesh, in_specs=in_specs, out_specs=out_specs, check_vma=False)
```

profile of v0, /device:TPU:1, one launch (start us, length us, event | category | flops | bytes accessed | tf_op | source)
XLA Modules:
  0.0 1105.9 jit_solution(4509234009213822228)
XLA Ops:
  83.0 13.8 %gather_fusion = bf16[4096,32]{1,0:T(8,128)(2,1)S(1)} fusion(bf16[32,16384]{0,1:T(8,128)(2,1)} %bitcast.222, s32[4096]{0:T(1024)S(1)} %broadcast_clamp_fusion), kind=kCustom, calls=%fused_computation | custom fusion | bytes 540672 | tf_op jit(solution)/shard_map/jit(_take)/gather | solution.py:88
  99.6 14.2 %all-to-all-start = ((bf16[32,32,128]{2,0,1:T(8,128)(2,1)}), bf16[32,32,128]{2,0,1:T(8,128)(2,1)S(1)}, u32[]{:S(2)}, u32[]{:S(2)}) async-start(bf16[32,32,128]{2,0,1:T(8,128)(2,1)} %broadcast_select_fusion), calls=%async_computation | async-start | bytes 524288 | tf_op jit(solution)/shard_map/all_to_all | solution.py:91
  113.9 17.0 %all-to-all-done = bf16[32,32,128]{2,0,1:T(8,128)(2,1)S(1)} async-done(((bf16[32,32,128]{2,0,1:T(8,128)(2,1)}), bf16[32,32,128]{2,0,1:T(8,128)(2,1)S(1)}, u32[]{:S(2)}, u32[]{:S(2)}) %all-to-all-start) | async-done | bytes 262176 | tf_op jit(solution)/shard_map/all_to_all | solution.py:91
  131.0 68.3 %psum.35 = f32[4096]{0:T(1024)S(1)} all-reduce(f32[4096]{0:T(1024)S(1)} %bitcast.231), channel_id=1, replica_groups=mesh['grid'=32,'member'=16] {'member'}, use_global_device_ids=true, to_apply=%region_1.2 | all-reduce | flops 4096 | bytes 32768 | tf_op jit(solution)/shard_map/psum | solution.py:102
  200.2 176.4 %while.18 = (s32[]{:T(128)}, bf16[32,4096]{1,0:T(8,128)(2,1)S(1)}, f32[32,512]{1,0:T(8,128)S(1)}, bf16[32,4096]{1,0:T(8,128)(2,1)S(1)}, s32[]{:T(128)}, /*index=...) while((s32[]{:T(128)}, bf16[32,4096]{1,0:T(8,128)(2,1)S(1)}, ...), condition=%wide.region_3.4_spmd, body=%wide.region_2.3_spmd.sunk | while | flops 8388626 | bytes 2109760 | solution.py:120
  223.4 9.3 collective-permute-done
  235.2 9.4 collective-permute-done
  247.1 9.2 collective-permute-done
  258.8 9.5 collective-permute-done
  271.0 9.3 collective-permute-done
  282.9 9.3 collective-permute-done
  294.9 9.2 collective-permute-done
  306.7 9.5 collective-permute-done
  318.8 9.4 collective-permute-done
  330.7 9.3 collective-permute-done
  342.7 9.2 collective-permute-done
  354.5 9.5 collective-permute-done
  366.5 9.4 collective-permute-done
  377.3 212.3 %all-reduce.17.cloned.1.call-done = f32[32,512]{1,0:T(8,128)} async-done(((f32[32,512]{1,0:T(8,128)}), f32[32,512]{1,0:T(8,128)}) %all-reduce.17.cloned.1.call-update) | async-done | bytes 65552 | tf_op jit(solution)/shard_map/psum | solution.py:121
  595.1 47.7 %psum.37 = f32[32]{0:T(128)S(1)} all-reduce(f32[32]{0:T(128)S(1)} %convolution_bitcast_fusion.8), channel_id=1, replica_groups=mesh['grid'=32,'member'=16] {'grid'}, use_global_device_ids=true, to_apply=%region_13.14 | all-reduce | flops 32 | bytes 256 | tf_op jit(solution)/shard_map/psum | solution.py:121
  643.0 70.8 %all-reduce.13 = f32[512]{0:T(512)} all-reduce(f32[512]{0:T(512)S(1)} %dynamic-update-slice.23), channel_id=1, replica_groups=mesh['grid'=32,'member'=16] {'member'}, use_global_device_ids=true, to_apply=%add.13 | all-reduce | flops 512 | bytes 4096
  721.5 11.7 %cholesky.103 = f32[128,128]{1,0:T(8,128)S(1)} custom-call(f32[128,128]{1,0:T(8,128)S(1)} %cholesky.263), custom_call_target="Cholesky" | custom-call | tf_op jit(solution)/shard_map/jit(cholesky)/cholesky | solution.py:57
  733.8 9.8 custom-call.32
  746.8 11.7 %cholesky.215 = f32[128,128]{1,0:T(8,128)S(1)} custom-call(f32[128,128]{1,0:T(8,128)S(1)} %cholesky.267), custom_call_target="Cholesky" | custom-call | tf_op jit(solution)/shard_map/jit(cholesky)/cholesky | solution.py:57
  761.5 10.8 custom-call.33
  778.0 12.5 %cholesky.236 = f32[128,128]{1,0:T(8,128)S(1)} custom-call(f32[128,128]{1,0:T(8,128)} %cholesky.272), custom_call_target="Cholesky" | custom-call | tf_op jit(solution)/shard_map/jit(cholesky)/cholesky | solution.py:57
  793.3 10.6 custom-call.34
  807.0 12.7 %cholesky.253 = f32[128,128]{1,0:T(8,128)S(1)} custom-call(f32[128,128]{1,0:T(8,128)} %convolution_subtract_fusion.2), custom_call_target="Cholesky" | custom-call | tf_op jit(solution)/shard_map/jit(cholesky)/cholesky | solution.py:57
  830.8 14.3 %while.19 = (s32[]{:T(128)}, f32[512,512]{0,1:T(8,128)}, s32[4,2]{0,1:T(2,128)S(1)}, f32[4,128,128]{2,1,0:T(8,128)}, s32[]{:T(128)}) while((s32[]{:T(128)}, f32[512,512]{0,1:T(8,128)}, s32[4,2]{0,1:T(2,128)S(1)}, f32[4,128,128]{2,1,0:T(8,128)}, s32[]{:T(128)}) %tuple.85), condition=%wide.while_cond, body=%wide.while_body.sunk | while | flops 2 | bytes 393829 | solution.py:60
  845.2 40.1 %custom-call.35 = f32[4,128,128]{1,2,0:T(8,128)S(1)} custom-call(f32[4,128,128]{2,1,0:T(8,128)} %get-tuple-element.145), custom_call_target="InvertDiagBlocksLowerTriangular" | custom-call | tf_op jit(solution)/shard_map/triangular_solve | solution.py:60
  896.4 59.6 %psum.39 = f32[4096]{0:T(1024)S(1)} all-reduce(f32[4096]{0:T(1024)S(1)} %bitcast.235), channel_id=1, replica_groups=mesh['grid'=32,'member'=16] {'member'}, use_global_device_ids=true, to_apply=%region_20.21 | all-reduce | flops 4096 | bytes 32768 | tf_op jit(solution)/shard_map/psum | solution.py:138
  961.8 135.9 %all-reduce.19.cloned.1.call-done = f32[16,1024]{1,0:T(8,128)} async-done(((f32[16,1024]{1,0:T(8,128)}), f32[16,1024]{1,0:T(8,128)}) %all-reduce.19.cloned.1.call-update) | async-done | bytes 65552 | tf_op jit(solution)/shard_map/psum | solution.py:138
  (256 shorter events, 203.3 us)
Async XLA Ops:
  9.1 6.5 collective-permute-start.1
  13.5 5.9 collective-permute-start.2
  21.0 5.9 collective-permute-start.3
  25.0 7.2 collective-permute-start.4
  33.9 6.0 collective-permute-start.5
  38.0 5.7 collective-permute-start.6
  45.4 6.1 collective-permute-start.7
  49.5 6.2 collective-permute-start.8
  57.4 6.9 collective-permute-start.10
  58.7 7.1 collective-permute-start.9
  67.5 5.7 collective-permute-start.11
  71.3 6.3 collective-permute-start.12
  99.6 31.3 %all-to-all-start = ((bf16[32,32,128]{2,0,1:T(8,128)(2,1)}), bf16[32,32,128]{2,0,1:T(8,128)(2,1)S(1)}, u32[]{:S(2)}, u32[]{:S(2)}) async-start(bf16[32,32,128]{2,0,1:T(8,128)(2,1)} %broadcast_select_fusion), calls=%async_computation | async-start | bytes 524288 | tf_op jit(solution)/shard_map/all_to_all | solution.py:91
  113.8 475.7 %all-reduce.17.cloned.1.call-start = ((), (), s32[]{:S(2)}) async-start(), calls=%async_computation.1 | async-start | bytes 131072 | tf_op jit(solution)/shard_map/psum | solution.py:121
  200.2 8.8 collective-permute-start
  209.5 11.3 %collective-permute-start = (bf16[32,4096]{1,0:T(8,128)(2,1)S(1)}, bf16[32,4096]{1,0:T(8,128)(2,1)S(1)}, u32[]{:S(2)}, u32[]{:S(2)}) collective-permute-start(bf16[32,4096]{1,0:T(8,128)(2,1)S(1)} %get-tuple-element.301), channel_id=1, source_target_pairs={{0,1},{1,2},{2,3},{3,4},{4,5},{5,6},{6,7},{7,8},{8,9},{9,10},{10,1... | collective-permute-start | bytes 786440 | tf_op jit(solution)/shard_map/while/body/eval_jaxpr/ppermute | solution.py:32
  221.4 11.3 %collective-permute-start = (bf16[32,4096]{1,0:T(8,128)(2,1)S(1)}, bf16[32,4096]{1,0:T(8,128)(2,1)S(1)}, u32[]{:S(2)}, u32[]{:S(2)}) collective-permute-start(bf16[32,4096]{1,0:T(8,128)(2,1)S(1)} %get-tuple-element.301), channel_id=1, source_target_pairs={{0,1},{1,2},{2,3},{3,4},{4,5},{5,6},{6,7},{7,8},{8,9},{9,10},{10,1... | collective-permute-start | bytes 786440 | tf_op jit(solution)/shard_map/while/body/eval_jaxpr/ppermute | solution.py:32
  233.3 11.3 %collective-permute-start = (bf16[32,4096]{1,0:T(8,128)(2,1)S(1)}, bf16[32,4096]{1,0:T(8,128)(2,1)S(1)}, u32[]{:S(2)}, u32[]{:S(2)}) collective-permute-start(bf16[32,4096]{1,0:T(8,128)(2,1)S(1)} %get-tuple-element.301), channel_id=1, source_target_pairs={{0,1},{1,2},{2,3},{3,4},{4,5},{5,6},{6,7},{7,8},{8,9},{9,10},{10,1... | collective-permute-start | bytes 786440 | tf_op jit(solution)/shard_map/while/body/eval_jaxpr/ppermute | solution.py:32
  245.2 11.2 %collective-permute-start = (bf16[32,4096]{1,0:T(8,128)(2,1)S(1)}, bf16[32,4096]{1,0:T(8,128)(2,1)S(1)}, u32[]{:S(2)}, u32[]{:S(2)}) collective-permute-start(bf16[32,4096]{1,0:T(8,128)(2,1)S(1)} %get-tuple-element.301), channel_id=1, source_target_pairs={{0,1},{1,2},{2,3},{3,4},{4,5},{5,6},{6,7},{7,8},{8,9},{9,10},{10,1... | collective-permute-start | bytes 786440 | tf_op jit(solution)/shard_map/while/body/eval_jaxpr/ppermute | solution.py:32
  256.8 11.5 %collective-permute-start = (bf16[32,4096]{1,0:T(8,128)(2,1)S(1)}, bf16[32,4096]{1,0:T(8,128)(2,1)S(1)}, u32[]{:S(2)}, u32[]{:S(2)}) collective-permute-start(bf16[32,4096]{1,0:T(8,128)(2,1)S(1)} %get-tuple-element.301), channel_id=1, source_target_pairs={{0,1},{1,2},{2,3},{3,4},{4,5},{5,6},{6,7},{7,8},{8,9},{9,10},{10,1... | collective-permute-start | bytes 786440 | tf_op jit(solution)/shard_map/while/body/eval_jaxpr/ppermute | solution.py:32
  269.0 11.3 %collective-permute-start = (bf16[32,4096]{1,0:T(8,128)(2,1)S(1)}, bf16[32,4096]{1,0:T(8,128)(2,1)S(1)}, u32[]{:S(2)}, u32[]{:S(2)}) collective-permute-start(bf16[32,4096]{1,0:T(8,128)(2,1)S(1)} %get-tuple-element.301), channel_id=1, source_target_pairs={{0,1},{1,2},{2,3},{3,4},{4,5},{5,6},{6,7},{7,8},{8,9},{9,10},{10,1... | collective-permute-start | bytes 786440 | tf_op jit(solution)/shard_map/while/body/eval_jaxpr/ppermute | solution.py:32
  281.0 11.3 %collective-permute-start = (bf16[32,4096]{1,0:T(8,128)(2,1)S(1)}, bf16[32,4096]{1,0:T(8,128)(2,1)S(1)}, u32[]{:S(2)}, u32[]{:S(2)}) collective-permute-start(bf16[32,4096]{1,0:T(8,128)(2,1)S(1)} %get-tuple-element.301), channel_id=1, source_target_pairs={{0,1},{1,2},{2,3},{3,4},{4,5},{5,6},{6,7},{7,8},{8,9},{9,10},{10,1... | collective-permute-start | bytes 786440 | tf_op jit(solution)/shard_map/while/body/eval_jaxpr/ppermute | solution.py:32
  293.0 11.2 %collective-permute-start = (bf16[32,4096]{1,0:T(8,128)(2,1)S(1)}, bf16[32,4096]{1,0:T(8,128)(2,1)S(1)}, u32[]{:S(2)}, u32[]{:S(2)}) collective-permute-start(bf16[32,4096]{1,0:T(8,128)(2,1)S(1)} %get-tuple-element.301), channel_id=1, source_target_pairs={{0,1},{1,2},{2,3},{3,4},{4,5},{5,6},{6,7},{7,8},{8,9},{9,10},{10,1... | collective-permute-start | bytes 786440 | tf_op jit(solution)/shard_map/while/body/eval_jaxpr/ppermute | solution.py:32
  304.7 11.4 %collective-permute-start = (bf16[32,4096]{1,0:T(8,128)(2,1)S(1)}, bf16[32,4096]{1,0:T(8,128)(2,1)S(1)}, u32[]{:S(2)}, u32[]{:S(2)}) collective-permute-start(bf16[32,4096]{1,0:T(8,128)(2,1)S(1)} %get-tuple-element.301), channel_id=1, source_target_pairs={{0,1},{1,2},{2,3},{3,4},{4,5},{5,6},{6,7},{7,8},{8,9},{9,10},{10,1... | collective-permute-start | bytes 786440 | tf_op jit(solution)/shard_map/while/body/eval_jaxpr/ppermute | solution.py:32
  316.8 11.3 %collective-permute-start = (bf16[32,4096]{1,0:T(8,128)(2,1)S(1)}, bf16[32,4096]{1,0:T(8,128)(2,1)S(1)}, u32[]{:S(2)}, u32[]{:S(2)}) collective-permute-start(bf16[32,4096]{1,0:T(8,128)(2,1)S(1)} %get-tuple-element.301), channel_id=1, source_target_pairs={{0,1},{1,2},{2,3},{3,4},{4,5},{5,6},{6,7},{7,8},{8,9},{9,10},{10,1... | collective-permute-start | bytes 786440 | tf_op jit(solution)/shard_map/while/body/eval_jaxpr/ppermute | solution.py:32
  328.8 11.3 %collective-permute-start = (bf16[32,4096]{1,0:T(8,128)(2,1)S(1)}, bf16[32,4096]{1,0:T(8,128)(2,1)S(1)}, u32[]{:S(2)}, u32[]{:S(2)}) collective-permute-start(bf16[32,4096]{1,0:T(8,128)(2,1)S(1)} %get-tuple-element.301), channel_id=1, source_target_pairs={{0,1},{1,2},{2,3},{3,4},{4,5},{5,6},{6,7},{7,8},{8,9},{9,10},{10,1... | collective-permute-start | bytes 786440 | tf_op jit(solution)/shard_map/while/body/eval_jaxpr/ppermute | solution.py:32
  340.8 11.2 %collective-permute-start = (bf16[32,4096]{1,0:T(8,128)(2,1)S(1)}, bf16[32,4096]{1,0:T(8,128)(2,1)S(1)}, u32[]{:S(2)}, u32[]{:S(2)}) collective-permute-start(bf16[32,4096]{1,0:T(8,128)(2,1)S(1)} %get-tuple-element.301), channel_id=1, source_target_pairs={{0,1},{1,2},{2,3},{3,4},{4,5},{5,6},{6,7},{7,8},{8,9},{9,10},{10,1... | collective-permute-start | bytes 786440 | tf_op jit(solution)/shard_map/while/body/eval_jaxpr/ppermute | solution.py:32
  352.5 11.4 %collective-permute-start = (bf16[32,4096]{1,0:T(8,128)(2,1)S(1)}, bf16[32,4096]{1,0:T(8,128)(2,1)S(1)}, u32[]{:S(2)}, u32[]{:S(2)}) collective-permute-start(bf16[32,4096]{1,0:T(8,128)(2,1)S(1)} %get-tuple-element.301), channel_id=1, source_target_pairs={{0,1},{1,2},{2,3},{3,4},{4,5},{5,6},{6,7},{7,8},{8,9},{9,10},{10,1... | collective-permute-start | bytes 786440 | tf_op jit(solution)/shard_map/while/body/eval_jaxpr/ppermute | solution.py:32
  364.6 11.3 %collective-permute-start = (bf16[32,4096]{1,0:T(8,128)(2,1)S(1)}, bf16[32,4096]{1,0:T(8,128)(2,1)S(1)}, u32[]{:S(2)}, u32[]{:S(2)}) collective-permute-start(bf16[32,4096]{1,0:T(8,128)(2,1)S(1)} %get-tuple-element.301), channel_id=1, source_target_pairs={{0,1},{1,2},{2,3},{3,4},{4,5},{5,6},{6,7},{7,8},{8,9},{9,10},{10,1... | collective-permute-start | bytes 786440 | tf_op jit(solution)/shard_map/while/body/eval_jaxpr/ppermute | solution.py:32
  377.2 336.6 %all-gather.2.cloned.1.call-start = ((), (), s32[]{:S(2)}) async-start(), calls=%async_computation.2 | async-start | bytes 1114112 | tf_op jit(solution)/shard_map/all_gather | solution.py:123
  589.6 508.1 %all-reduce.19.cloned.1.call-start = ((), (), s32[]{:S(2)}) async-start(), calls=%async_computation.3 | async-start | bytes 131072 | tf_op jit(solution)/shard_map/psum | solution.py:138
  896.0 203.1 %copy-start.19 = (f32[512,1]{0,1:T(1,128)}, f32[512,1]{0,1:T(1,128)S(1)}, u32[]{:S(2)}) copy-start(f32[512,1]{0,1:T(1,128)S(1)} %pad_maximum_fusion.12) | copy-start | bytes 6148
  (24 other events, 843.3 us)
Sparse Core Ops, SparseCore 0:
  377.3 212.1 all-reduce.16
  593.4 80.5 all-gather.1
  961.3 136.3 all-reduce.18
where the time goes:
time: 1120 us; the launch traced here: 1110 us
  waiting for transfers between devices  526 us (47%)
  blocking collectives  246 us (22%)
  other arithmetic  150 us (13%)
  starting transfers between devices  78.8 us (7%)
  local copies, waits for them, and re-layouts  59.7 us (5%)
  matrix products  23.3 us (2%)
  between operations  20.4 us (2%)
    psum x1, waiting for transfers between devices, local(): row_block, right_rows = lax.psum((row_block, right_rows), 'grid')  212 us
    psum x1, waiting for transfers between devices, local(): lax.psum((field_contribution, slot_term), 'member')  136 us
    ppermute x15, waiting for transfers between devices, shifted(): return lax.ppermute(value, axis, pairs)  135 us
    another operation x15, other arithmetic, solve_weights(): factor = jnp.linalg.cholesky(system)  88.5 us
    unnamed x1, blocking collectives  70.8 us
    psum x1, blocking collectives, local(): obs_mean = lax.psum(jnp.sum(sampled_float, axis=0), 'member') / sample_count  68.3 us
    psum x1, blocking collectives, local(): lax.psum((field_contribution, slot_term), 'member')  59.6 us
    psum x1, blocking collectives, local(): row_block, right_rows = lax.psum((row_block, right_rows), 'grid')  47.7 us
  transfers between devices with their start and end apart: 31, of which 29 were waited for; matrix products, arithmetic and copies ran while one was open for 1% of the time, Pallas kernels for 0%

commit v1 on v0

v1 whole, which is shorter than its diff:
```python
import functools

import jax
import jax.numpy as jnp
from jax import lax
from jax.experimental import pallas as pl
from jax.experimental.pallas import tpu as pltpu
from jax.sharding import PartitionSpec as P

STEPS = 6
MEMBERS = 512
HALO = 6
EXT = 28
NC = 1024
HIGH = lax.Precision.HIGHEST
MESH = pl.DeviceIdType.MESH
F32 = jnp.float32
BF16 = jnp.bfloat16
VMEM_LIMIT = 56 * 1024 * 1024


def place():
    g = lax.axis_index("grid")
    m = lax.axis_index("member")
    return g, m


def plane_of(g, m):
    return (g // 16) * 8 + (m // 8) * 4 + (m // 2) % 4


def plane_peer(p, g, m):
    return (p // 8) * 16 + g % 16, ((p // 4) % 2) * 8 + (p % 4) * 2 + m % 2


def z_reducer(j):
    return (8 * j) // 3


def remote(src, dst, send, recv, where):
    return pltpu.make_async_remote_copy(
        src_ref=src, dst_ref=dst, send_sem=send, recv_sem=recv, device_id=where, device_id_type=MESH
    )


def signal(sem, where):
    pl.semaphore_signal(sem, inc=1, device_id=where, device_id_type=MESH)


def split3(value):
    a = value.astype(BF16)
    rest = value - a.astype(F32)
    b = rest.astype(BF16)
    c = (rest - b.astype(F32)).astype(BF16)
    return a, b, c


def fill_coefs(g, cce, dif, vel, coef):
    for half in range(4):
        rows = pl.ds(half * 8, 8)
        cls = cce[rows, :]
        d = jnp.zeros((8, NC), F32)
        vx = jnp.zeros((8, NC), F32)
        vy = jnp.zeros((8, NC), F32)
        for c in range(16):
            hit = cls == c
            d = jnp.where(hit, dif[c], d)
            vx = jnp.where(hit, vel[0, c], vx)
            vy = jnp.where(hit, vel[1, c], vy)
        row = lax.broadcasted_iota(jnp.int32, (8, NC), 0) + (half * 8 - 8) + g * 16
        col = lax.broadcasted_iota(jnp.int32, (8, NC), 1)
        inside = jnp.logical_and(row >= 0, row < 512)
        coef[0, rows, :] = jnp.where(inside, 1.0 - 4.0 * d, 0.0)
        coef[1, rows, :] = jnp.where(inside, d + 0.5 * vy, 0.0)
        coef[2, rows, :] = jnp.where(inside, d - 0.5 * vy, 0.0)
        coef[3, rows, :] = jnp.where(jnp.logical_and(inside, col > 0), d + 0.5 * vx, 0.0)
        coef[4, rows, :] = jnp.where(jnp.logical_and(inside, col < NC - 1), d - 0.5 * vx, 0.0)


def stencil(src, r, q, c):
    sl = pl.ds(q * 8, 8)
    mid = src[r, sl, :]
    out = c[0] * mid
    out = out + c[1] * src[r - 1, sl, :] + c[2] * src[r + 1, sl, :]
    return out + c[3] * pltpu.roll(mid, 1, 1) + c[4] * pltpu.roll(mid, NC - 1, 1)


def main_kernel(
    stop, x_ref, cc_ref, dif, vel, cells, wv, pred, ff, samples,
    turn, a_buf, b_buf, coef, pbf, cce, hsend, hrecv, wrecv, sbuf, fpart, rcore, rplane, zsend, zrecv, fin,
    s_halo, r_halo, s_cls, r_cls, s_w, r_w, s_s, r_s, s_c, r_c, s_p, r_p, s_z, r_z, s_g, r_g, s_a, r_a, s_b, r_b,
):
    g, m = place()
    z, xl = g % 16, g // 16
    core = m % 2
    p = plane_of(g, m)
    other = m + 1 - 2 * core
    sender = g // 2 == m
    barrier = pltpu.get_barrier_semaphore()

    @pl.when(g > 0)
    def _():
        signal(barrier, (g - 1, m))

    @pl.when(g < 31)
    def _():
        signal(barrier, (g + 1, m))

    for o in range(2):
        @pl.when(2 * m + o != g)
        def _(o=o):
            signal(barrier, (2 * m + o, m))

    def greet(d, carry):
        signal(barrier, (g, (m + d) % 16))
        signal(barrier, plane_peer((p + d) % 16, g, m))
        signal(barrier, (xl * 16 + (z + d) % 16, m))
        return carry

    lax.fori_loop(1, 16, greet, 0)

    def unpack(i, carry):
        value = x_ref[i].astype(F32)
        for t in range(8):
            turn[t, pl.ds(i * 16, 16), :] = value[:, t * 128:(t + 1) * 128]
        return carry

    lax.fori_loop(0, 32, unpack, 0)

    def shuffle(r, carry):
        for q in range(4):
            for t in range(8):
                a_buf[r + HALO, pl.ds(q * 8, 8), t * 128:(t + 1) * 128] = turn[t, pl.ds(q * 128 + r, 8, stride=16), :]
        return carry

    lax.fori_loop(0, 16, shuffle, 0)
    for side in range(2):
        def pack(r, carry, side=side):
            hsend[side, r] = a_buf[r + HALO + side * 10].astype(BF16)
            return carry

        lax.fori_loop(0, HALO, pack, 0)

    count = 45 + (g > 0).astype(jnp.int32) + (g < 31).astype(jnp.int32) + 31 * sender.astype(jnp.int32)
    pl.semaphore_wait(barrier, count)

    up = remote(hsend.at[0], hrecv.at[1], s_halo.at[0], r_halo.at[1], (g - 1, m))
    down = remote(hsend.at[1], hrecv.at[0], s_halo.at[1], r_halo.at[0], (g + 1, m))
    cup = remote(cc_ref.at[pl.ds(0, 8)], cce.at[pl.ds(24, 8)], s_cls.at[0], r_cls.at[1], (g - 1, m))
    cdown = remote(cc_ref.at[pl.ds(8, 8)], cce.at[pl.ds(0, 8)], s_cls.at[1], r_cls.at[0], (g + 1, m))

    @pl.when(g > 0)
    def _():
        cup.start()
        up.start()

    @pl.when(g < 31)
    def _():
        cdown.start()
        down.start()

    @pl.when(sender)
    def _():
        def give(d, carry):
            s = (g + d) % 32
            remote(wv.at[s], wrecv.at[g % 2], s_w.at[d], r_w.at[g % 2], (s, m)).start()
            return carry

        lax.fori_loop(1, 32, give, 0)
        wrecv[g % 2] = wv[g]

    cce[pl.ds(8, 16), :] = cc_ref[...]

    @pl.when(g == 0)
    def _():
        hrecv[0] = jnp.zeros((HALO, 32, NC), BF16)
        cce[pl.ds(0, 8), :] = jnp.zeros((8, NC), jnp.int32)

    @pl.when(g == 31)
    def _():
        hrecv[1] = jnp.zeros((HALO, 32, NC), BF16)
        cce[pl.ds(24, 8), :] = jnp.zeros((8, NC), jnp.int32)

    @pl.when(g > 0)
    def _():
        cup.wait_send()
        cdown.wait_recv()
        up.wait_send()
        down.wait_recv()

    @pl.when(g < 31)
    def _():
        cdown.wait_send()
        cup.wait_recv()
        down.wait_send()
        up.wait_recv()

    fill_coefs(g, cce, dif, vel, coef)
    for side in range(2):
        def widen(r, carry, side=side):
            a_buf[r + side * 22] = hrecv[side, r].astype(F32)
            return carry

        lax.fori_loop(0, HALO, widen, 0)

    bufs = (a_buf, b_buf)
    for k in range(STEPS):
        src, dst = bufs[k % 2], bufs[(k + 1) % 2]

        def line(r, carry, src=src, dst=dst, k=k):
            c = [jnp.broadcast_to(coef[i, pl.ds(r + 2, 1), :], (8, NC)) for i in range(5)]
            rows = []
            for q in range(4):
                out = stencil(src, r, q, c)
                if k < STEPS - 1:
                    dst[r, pl.ds(q * 8, 8), :] = out
                else:
                    for t in range(8):
                        turn[t, pl.ds(q * 128 + r - HALO, 8, stride=16), :] = out[:, t * 128:(t + 1) * 128]
                    rows.append(out)
            if k == STEPS - 1:
                pbf[pl.ds((r - HALO) * 32, 32), :] = jnp.concatenate(rows, axis=0).astype(BF16)
            return carry

        lax.fori_loop(k + 1, EXT - 1 - k, line, 0)

    def finish(i, carry):
        for t in range(8):
            pred[i, :, t * 128:(t + 1) * 128] = turn[t, pl.ds(i * 16, 16), :].astype(BF16)
        return carry

    lax.fori_loop(0, 32, finish, 0)

    def sample(chunk):
        cell = cells[chunk]
        col = cell & (NC - 1)
        row = cell >> 10
        onehot = (lax.broadcasted_iota(jnp.int32, (NC, 256), 0) == col).astype(F32).astype(BF16)
        wide = jnp.dot(pbf[...], onehot, preferred_element_type=F32)
        total = jnp.zeros((32, 256), F32)
        for r in range(16):
            total = total + jnp.where(row == r, wide[r * 32:(r + 1) * 32], 0.0)
        return total.astype(BF16)

    def scatter(d, carry):
        peer = (m + d) % 16
        sbuf[d] = sample(peer)
        remote(sbuf.at[d], samples.at[m], s_s.at[d], r_s.at[m], (g, peer)).start()
        return carry

    lax.fori_loop(1, 16, scatter, 0)
    samples[m] = sample(m)

    @pl.when(sender)
    def _():
        def given(d, carry):
            remote(wv.at[g], wrecv.at[g % 2], s_w.at[d], r_w.at[g % 2], (g, m)).wait_send()
            return carry

        lax.fori_loop(1, 32, given, 0)

    for o in range(2):
        @pl.when(2 * m + o != g)
        def _(o=o):
            remote(wv.at[g], wrecv.at[o], s_w.at[0], r_w.at[o], (g, m)).wait_recv()

    def scattered(d, carry):
        peer = (m + d) % 16
        c = remote(sbuf.at[d], samples.at[peer], s_s.at[d], r_s.at[peer], (g, peer))
        c.wait_send()
        c.wait_recv()
        return carry

    lax.fori_loop(1, 16, scattered, 0)

    sampled = samples[...].reshape(MEMBERS, 256).astype(F32)
    mean = jnp.sum(sampled, axis=0, keepdims=True) / MEMBERS
    weight = jnp.concatenate([wrecv[0, :, 0:128], wrecv[1, :, 0:128]], axis=1)
    value = jnp.concatenate([wrecv[0, :, 128:256], wrecv[1, :, 128:256]], axis=1)
    panel = ((sampled - mean) * weight).astype(BF16)
    dep = (value - mean) * weight
    parts = split3(dep)
    line_at = lax.broadcasted_iota(jnp.int32, (128, 256), 0)
    dep_one = jnp.zeros((128, 256), F32)
    dep_two = jnp.zeros((128, 256), F32)
    for i in range(3):
        dep_one = jnp.where(line_at == i, parts[i].astype(F32), dep_one)
        dep_two = jnp.where(line_at == 64 + i, parts[i].astype(F32), dep_two)
    dep_one = dep_one.astype(BF16)
    dep_two = dep_two.astype(BF16)
    blk = [panel[i * 128:(i + 1) * 128] for i in range(4)]

    def outer(a, b):
        return lax.dot_general(a, b, (((1,), (1,)), ((), ())), preferred_element_type=F32)

    pairs = (
        ((0, 0), (0, 1), (0, 2), (0, 3), (3, 3)),
        ((1, 1), (1, 2), (1, 3), (2, 2), (2, 3)),
    )
    for h in range(2):
        for t in range(5):
            i, j = pairs[h][t]
            fpart[h, :, t] = outer(blk[i], blk[j]).reshape(16, 8, 128)
        fpart[h, :, 5] = (outer(blk[h], dep_one) + outer(blk[3 - h], dep_two)).reshape(16, 8, 128)

    swap = remote(fpart.at[1 - core], rcore, s_c.at[0], r_c.at[0], (g, other))
    swap.start()
    swap.wait()

    def pair_sum(i, carry):
        rcore[i] = rcore[i] + fpart[core, i]
        return carry

    lax.fori_loop(0, 16, pair_sum, 0)

    def plane_give(d, carry):
        q = (p + d) % 16
        remote(rcore.at[q], rplane.at[p], s_p.at[d], r_p.at[p], plane_peer(q, g, m)).start()
        return carry

    lax.fori_loop(1, 16, plane_give, 0)

    def plane_take(d, total):
        q = (p + d) % 16
        c = remote(rcore.at[q], rplane.at[q], s_p.at[d], r_p.at[q], plane_peer(q, g, m))
        c.wait_recv()
        return total + rplane[q]

    zsend[...] = lax.fori_loop(1, 16, plane_take, rcore[p])

    for j in range(6):
        @pl.when(z != z_reducer(j))
        def _(j=j):
            remote(zsend.at[j], zrecv.at[z], s_z.at[j], r_z.at[z], (xl * 16 + z_reducer(j), m)).start()

    for j in range(6):
        @pl.when(z == z_reducer(j))
        def _(j=j):
            def z_take(d, total):
                q = (z + d) % 16
                remote(zsend.at[j], zrecv.at[q], s_z.at[j], r_z.at[q], (xl * 16 + q, m)).wait_recv()
                return total + zrecv[q]

            fin[p, j] = lax.fori_loop(1, 16, z_take, zsend[j])

            def z_give(d, carry):
                q = (z + d) % 16
                remote(fin.at[p, j], fin.at[p, j], s_g.at[d], r_g.at[j], (xl * 16 + q, m)).start()
                return carry

            lax.fori_loop(1, 16, z_give, 0)

    for j in range(6):
        @pl.when(z != z_reducer(j))
        def _(j=j):
            remote(fin.at[p, j], fin.at[p, j], s_g.at[0], r_g.at[j], (xl * 16 + z_reducer(j), m)).wait_recv()

    def plane_send(d, carry):
        q = (p + d) % 16
        remote(fin.at[p], fin.at[p], s_a.at[d], r_a.at[p], plane_peer(q, g, m)).start()
        return carry

    lax.fori_loop(1, 16, plane_send, 0)

    def plane_got(d, carry):
        q = (p + d) % 16
        remote(fin.at[q], fin.at[q], s_a.at[d], r_a.at[q], plane_peer(q, g, m)).wait_recv()
        return carry

    lax.fori_loop(1, 16, plane_got, 0)
    back = remote(fin, ff.at[core], s_b.at[0], r_b.at[0], (g, other))
    back.start()

    def keep(i, carry):
        ff[core, i] = fin[i]
        return carry

    lax.fori_loop(0, 16, keep, 0)
    back.wait()

    def drain(d, carry):
        q = (p + d) % 16
        remote(rcore.at[q], rplane.at[q], s_p.at[d], r_p.at[q], plane_peer(q, g, m)).wait_send()
        remote(fin.at[p], fin.at[p], s_a.at[d], r_a.at[p], plane_peer(q, g, m)).wait_send()
        return carry

    lax.fori_loop(1, 16, drain, 0)
    for j in range(6):
        @pl.when(z != z_reducer(j))
        def _(j=j):
            remote(zsend.at[j], zrecv.at[z], s_z.at[j], r_z.at[z], (xl * 16 + z_reducer(j), m)).wait_send()

        @pl.when(z == z_reducer(j))
        def _(j=j):
            def z_given(d, carry):
                q = (z + d) % 16
                remote(fin.at[p, j], fin.at[p, j], s_g.at[d], r_g.at[j], (xl * 16 + q, m)).wait_send()
                return carry

            lax.fori_loop(1, 16, z_given, 0)


def run_main(x, cc, dif, vel, cells, wv, stop=None):
    vmem = pl.BlockSpec(memory_space=pltpu.VMEM)
    smem = pl.BlockSpec(memory_space=pltpu.SMEM)
    dma = pltpu.SemaphoreType.DMA
    return pl.pallas_call(
        functools.partial(main_kernel, stop),
        out_shape=(
            jax.ShapeDtypeStruct((32, 16, NC), BF16),
            jax.ShapeDtypeStruct((2, 16, 6, 8, 128), F32),
            jax.ShapeDtypeStruct((16, 32, 256), BF16),
        ),
        in_specs=[vmem, vmem, smem, smem, vmem, vmem],
        out_specs=(vmem, vmem, vmem),
        scratch_shapes=[
            pltpu.VMEM((8, 512, 128), F32),
            pltpu.VMEM((EXT, 32, NC), F32),
            pltpu.VMEM((EXT, 32, NC), F32),
            pltpu.VMEM((5, 32, NC), F32),
            pltpu.VMEM((512, NC), BF16),
            pltpu.VMEM((32, NC), jnp.int32),
            pltpu.VMEM((2, HALO, 32, NC), BF16),
            pltpu.VMEM((2, HALO, 32, NC), BF16),
            pltpu.VMEM((2, 1, 256), F32),
            pltpu.VMEM((16, 32, 256), BF16),
            pltpu.VMEM((2, 16, 6, 8, 128), F32),
            pltpu.VMEM((16, 6, 8, 128), F32),
            pltpu.VMEM((16, 6, 8, 128), F32),
            pltpu.VMEM((6, 8, 128), F32),
            pltpu.VMEM((16, 8, 128), F32),
            pltpu.VMEM((16, 6, 8, 128), F32),
            dma((2,)), dma((2,)), dma((2,)), dma((2,)), dma((32,)), dma((2,)), dma((16,)), dma((16,)),
            dma((1,)), dma((1,)), dma((16,)), dma((16,)), dma((6,)), dma((16,)), dma((16,)), dma((6,)),
            dma((16,)), dma((16,)), dma((1,)), dma((1,)),
        ],
        compiler_params=pltpu.CompilerParams(
            collective_id=0, has_side_effects=True, vmem_limit_bytes=VMEM_LIMIT
        ),
    )(x, cc, dif, vel, cells, wv)


def inverse(a):
    row = lax.broadcasted_iota(jnp.int32, (128, 128), 0)
    col = lax.broadcasted_iota(jnp.int32, (128, 128), 1)
    diag = jnp.where(row == col, a, 0.0)
    s_col = lax.rsqrt(jnp.sum(diag, axis=1, keepdims=True))
    s_row = lax.rsqrt(jnp.sum(diag, axis=0, keepdims=True))
    lane = lax.broadcasted_iota(jnp.int32, (1, 128), 1)
    line = lax.broadcasted_iota(jnp.int32, (128, 1), 0)

    def sweep(_, a):
        for k in range(8):
            r = a[k:k + 1, :]
            c = a[:, k:k + 1]
            d = a[k:k + 1, k:k + 1]
            inv = 1.0 / d
            r = jnp.where(lane == k, 1.0 + inv, r * inv)
            c = jnp.where(line == k, d - 1.0, c)
            a = a - c * r
        a = jnp.concatenate([a[8:], a[:8]], axis=0)
        return pltpu.roll(a, 120, 1)

    a = lax.fori_loop(0, 16, sweep, a * s_col * s_row)
    return a * s_col * s_row


def mm(a, b):
    return jnp.dot(a, b, precision=HIGH, preferred_element_type=F32)


def solve_kernel(ff, xcol, xrow):
    row = lax.broadcasted_iota(jnp.int32, (128, 128), 0)
    col = lax.broadcasted_iota(jnp.int32, (128, 128), 1)
    ridge = jnp.where(row == col, float(MEMBERS - 1), 0.0)

    def tile(h, t):
        return ff[h, :, t].reshape(128, 128)

    def right(h, first):
        part = tile(h, 5)
        keep = jnp.logical_and(col >= first, col < first + 3)
        return jnp.broadcast_to(jnp.sum(jnp.where(keep, part, 0.0), axis=1, keepdims=True), (128, 128))

    a = {
        (0, 0): tile(0, 0), (0, 1): tile(0, 1), (0, 2): tile(0, 2), (0, 3): tile(0, 3), (3, 3): tile(0, 4),
        (1, 1): tile(1, 0), (1, 2): tile(1, 1), (1, 3): tile(1, 2), (2, 2): tile(1, 3), (2, 3): tile(1, 4),
    }
    b = [right(0, 0), right(1, 0), right(1, 64), right(0, 64)]
    w = {}
    y = []
    for k in range(4):
        d = inverse(a[k, k] + ridge)
        y.append(mm(d, b[k]))
        for j in range(k + 1, 4):
            w[k, j] = mm(d, a[k, j])
        for i in range(k + 1, 4):
            t = a[k, i].T
            b[i] = b[i] - mm(t, y[k])
            for j in range(i, 4):
                a[i, j] = a[i, j] - mm(t, w[k, j])
    x = [None] * 4
    for k in reversed(range(4)):
        total = y[k]
        for j in range(k + 1, 4):
            total = total - mm(w[k, j], x[j])
        x[k] = total
    for k in range(4):
        xcol[pl.ds(k * 128, 128), :] = x[k]
        xrow[:, k * 128:(k + 1) * 128] = x[k].T[0:8, :]


def run_solve(ff):
    vmem = pl.BlockSpec(memory_space=pltpu.VMEM)
    return pl.pallas_call(
        solve_kernel,
        out_shape=(jax.ShapeDtypeStruct((512, 128), F32), jax.ShapeDtypeStruct((8, 512), F32)),
        in_specs=[vmem],
        out_specs=(vmem, vmem),
        compiler_params=pltpu.CompilerParams(vmem_limit_bytes=VMEM_LIMIT),
    )(ff)


def final_kernel(
    xcol, xrow, pred, samples, mean_out, obs_out,
    part, rpart, gath, osend, orecv, s_r, r_r, s_g, r_g, s_o, r_o,
):
    g, m = place()
    barrier = pltpu.get_barrier_semaphore()

    def greet(d, carry):
        signal(barrier, (g, (m + d) % 16))
        return carry

    lax.fori_loop(1, 16, greet, 0)

    def greet_far(s, carry):
        @pl.when(jnp.logical_or(s != g, m != g // 2))
        def _():
            signal(barrier, (s, g // 2))
        return carry

    lax.fori_loop(0, 32, greet_far, 0)

    x_all = xcol[...]
    shift = 1.0 / MEMBERS - jnp.sum(x_all[:, 0:1], axis=0, keepdims=True) / MEMBERS
    mine = xcol[pl.ds(m * 32, 32), :][:, 0:1] + shift

    total = jnp.zeros((16, NC), F32)
    for i in range(32):
        total = total + mine[i:i + 1, 0:1] * pred[i].astype(F32)
    for r in range(16):
        part[r] = total[r:r + 1, :]
    coef_row = xrow[...] + shift
    slot = jnp.zeros((8, 256), F32)
    flat = samples[...].reshape(MEMBERS, 256)
    for piece in split3(coef_row):
        slot = slot + jnp.dot(piece, flat, preferred_element_type=F32)
    osend[0] = slot[0:1, 0:128]
    osend[1] = slot[0:1, 128:256]

    selfish = (g // 2 == m).astype(jnp.int32)
    pl.semaphore_wait(barrier, 47 - selfish)

    def give(d, carry):
        q = (m + d) % 16
        remote(part.at[q], rpart.at[m], s_r.at[d], r_r.at[m], (g, q)).start()
        return carry

    lax.fori_loop(1, 16, give, 0)

    def show(d, carry):
        o = 2 * m + d // 16
        q = d % 16

        @pl.when(jnp.logical_or(o != g, q != m))
        def _():
            remote(osend.at[d // 16], orecv.at[g], s_o.at[d], r_o.at[g], (o, q)).start()

        @pl.when(jnp.logical_and(o == g, q == m))
        def _():
            orecv[g] = osend[d // 16]
        return carry

    lax.fori_loop(0, 32, show, 0)

    def take(d, total):
        q = (m + d) % 16
        remote(part.at[q], rpart.at[q], s_r.at[d], r_r.at[q], (g, q)).wait_recv()
        return total + rpart[q]

    gath[m] = lax.fori_loop(1, 16, take, part[m])

    def spread(d, carry):
        q = (m + d) % 16
        remote(gath.at[m], gath.at[m], s_g.at[d], r_g.at[m], (g, q)).start()
        return carry

    lax.fori_loop(1, 16, spread, 0)

    def got(d, carry):
        q = (m + d) % 16
        remote(gath.at[q], gath.at[q], s_g.at[d], r_g.at[q], (g, q)).wait_recv()
        return carry

    lax.fori_loop(1, 16, got, 0)

    def seen(s, carry):
        @pl.when(jnp.logical_or(s != g, m != g // 2))
        def _():
            remote(osend.at[0], orecv.at[s], s_o.at[0], r_o.at[s], (s, g // 2)).wait_recv()
        return carry

    lax.fori_loop(0, 32, seen, 0)
    for r in range(16):
        mean_out[r:r + 1, :] = gath[r]
    for s in range(32):
        obs_out[s:s + 1, :] = orecv[s]

    def drain(d, carry):
        q = (m + d) % 16
        remote(part.at[q], rpart.at[q], s_r.at[d], r_r.at[q], (g, q)).wait_send()
        remote(gath.at[m], gath.at[m], s_g.at[d], r_g.at[m], (g, q)).wait_send()
        return carry

    lax.fori_loop(1, 16, drain, 0)

    def shown(d, carry):
        o = 2 * m + d // 16
        q = d % 16

        @pl.when(jnp.logical_or(o != g, q != m))
        def _():
            remote(osend.at[d // 16], orecv.at[g], s_o.at[d], r_o.at[g], (o, q)).wait_send()
        return carry

    lax.fori_loop(0, 32, shown, 0)


def run_final(xcol, xrow, pred, samples):
    vmem = pl.BlockSpec(memory_space=pltpu.VMEM)
    dma = pltpu.SemaphoreType.DMA
    return pl.pallas_call(
        final_kernel,
        out_shape=(jax.ShapeDtypeStruct((16, NC), F32), jax.ShapeDtypeStruct((32, 128), F32)),
        in_specs=[vmem] * 4,
        out_specs=(vmem, vmem),
        scratch_shapes=[
            pltpu.VMEM((16, 1, NC), F32),
            pltpu.VMEM((16, 1, NC), F32),
            pltpu.VMEM((16, 1, NC), F32),
            pltpu.VMEM((2, 1, 128), F32),
            pltpu.VMEM((32, 1, 128), F32),
            dma((16,)), dma((16,)), dma((16,)), dma((16,)), dma((32,)), dma((32,)),
        ],
        compiler_params=pltpu.CompilerParams(
            collective_id=1, has_side_effects=True, vmem_limit_bytes=VMEM_LIMIT
        ),
    )(xcol, xrow, pred, samples)


def local(
    prior_sample_matrix, cell_class, diffusion_table, velocity_table, obs_cells, obs_count, obs_value, obs_scale
):
    slot_index = jnp.arange(128, dtype=jnp.int32)
    valid = (slot_index[None, :] < obs_count[0][:, None]).astype(F32)
    wv = jnp.concatenate([obs_scale[0] * valid, obs_value[0]], axis=1).reshape(32, 1, 256)
    cells = obs_cells.reshape(16, 1, 256)
    pred, ff, samples = run_main(prior_sample_matrix, cell_class, diffusion_table, velocity_table, cells, wv)
    xcol, xrow = run_solve(ff)
    mean, obs = run_final(xcol, xrow, pred, samples)
    return pred, mean, obs.reshape(1, 32, 128), xrow[0]


def solution(mesh):
    in_specs = (
        P("member", "grid", None),
        P("grid", None),
        P(),
        P(),
        P("grid", None, None),
        P("grid", None),
        P("grid", None, None),
        P("grid", None, None),
    )
    out_specs = (P("member", "grid", None), P("grid", None), P("grid", None, None), P())
    return jax.shard_map(local, mesh=mesh, in_specs=in_specs, out_specs=out_specs, check_vma=False)
```

time: 1120 us -> 175 us (0.16); the launches traced: 1110 us -> 175 us
  waiting for transfers between devices: 526 us -> 0 us
  blocking collectives: 246 us -> 0 us
  Pallas kernels: 0 us -> 168 us
  other arithmetic: 150 us -> 0.8 us
  starting transfers between devices: 78.8 us -> 0 us
  local copies, waits for them, and re-layouts: 59.7 us -> 4.89 us
  matrix products: 23.3 us -> 0 us
  between operations: 20.4 us -> 0.67 us
    psum x2 -> x0, waiting for transfers between devices: 348 us -> none  [the longest x1 212 us: local(): row_block, right_rows = lax.psum((row_block, right_rows), 'grid')]
    psum x3 -> x0, blocking collectives: 176 us -> none  [the longest x1 68.3 us: local(): obs_mean = lax.psum(jnp.sum(sampled_float, axis=0), 'member') / sample_count]
    pallas_call x0 -> x3, Pallas kernels: none -> 168 us  [the longest x1 94.5 us: run_main(): pl.pallas_call(functools.partial(main_kernel, stop), out_shape=(jax.Shape...]
    ppermute x27 -> x0, waiting for transfers between devices: 161 us -> none  [the longest x15 135 us: shifted(): return lax.ppermute(value, axis, pairs)]
    another operation x19 -> x0, other arithmetic: 130 us -> none  [the longest x15 88.5 us: solve_weights(): factor = jnp.linalg.cholesky(system)]
    unnamed x1 -> x0, blocking collectives: 70.8 us -> none
    ppermute x27 -> x0, starting transfers between devices: 64.5 us -> none  [the longest x15 31.2 us: shifted(): return lax.ppermute(value, axis, pairs)]
    another operation x34 -> x0, local copies, waits for them, and re-layouts: 21 us -> none
  transfers between devices with their start and end apart: 31 -> 0, of which waited for: 29 -> 0; matrix products, arithmetic and copies ran while one was open for 1% -> 0% of each run, Pallas kernels for 0% -> 0%
where the time goes in v1:
time: 175 us
  Pallas kernels  168 us (96%)
  local copies, waits for them, and re-layouts  4.89 us (3%)
    pallas_call x1, Pallas kernels, run_main(): pl.pallas_call(functools.partial(main_kernel, stop), out_shape=(jax.Shape...  94.5 us
    pallas_call x1, Pallas kernels, run_solve(): pl.pallas_call(solve_kernel, out_shape=(jax.ShapeDtypeStruct((512, 128),...  53.7 us
    pallas_call x1, Pallas kernels, run_final(): pl.pallas_call(final_kernel, out_shape=(jax.ShapeDtypeStruct((16, NC), F3...  20 us

profile of v1, /device:TPU:1, one launch (start us, length us, event | category | flops | bytes accessed | tf_op | source)
XLA Modules:
  0.0 174.5 jit_solution(14013671636207231259)
XLA Ops:
  0.6 0.0 copy-start.4
  0.6 0.6 copy-done.4
  1.3 0.0 copy-start.3
  1.3 0.8 bitcast_select_fusion
  2.1 0.0 copy-done.3
  2.1 0.6 reshape.19.wv
  2.7 94.5 %shard_map.111 = (bf16[32,16,1024]{2,1,0:T(8,128)(2,1)}, f32[2,16,6,8,128]{4,3,2,1,0:T(8,128)}, bf16[16,32,256]{2,1,0:T(8,128)(2,1)}) custom-call(bf16[32,16,1024]{2,1,0:T(8,128)(2,1)} %x_ref.1, s32[16,1024]{1,0:T(8,128)} %cc_ref.1, f32[16]{0:T(128)} %dif.1, f32[2,16]{1,0:T(2,128)} %vel.1, s32[16,1,256]{2,1,0:T(1,128)} %bitcast.7, f32[32,1,256]{2,1,0:T(1,128)} %reshape.19.wv), custom_call_target="tpu_custom_call" | custom-call | tf_op jit(solution)/shard_map/pallas_call | solution.py:407
  97.2 0.0 copy-start
  97.2 53.7 %shard_map.112 = (f32[512,128]{1,0:T(8,128)}, f32[8,512]{1,0:T(8,128)}) custom-call(f32[2,16,6,8,128]{4,3,2,1,0:T(8,128)} %get-tuple-element.12.ff), custom_call_target="tpu_custom_call" | custom-call | tf_op jit(solution)/shard_map/pallas_call | solution.py:515
  150.9 20.0 %shard_map.113 = (f32[16,1024]{1,0:T(8,128)}, f32[32,128]{1,0:T(8,128)}) custom-call(f32[512,128]{1,0:T(8,128)} %get-tuple-element.13.xcol, f32[8,512]{1,0:T(8,128)} %get-tuple-element.14.xrow, bf16[32,16,1024]{2,1,0:T(8,128)(2,1)} %get-tuple-element.22.pred, bf16[16,32,256]{2,1,0:T(8,128)(2,1)} %get-tuple-element.15.samples), custom_call_target="tpu_custom_call" | custom-call | tf_op jit(solution)/shard_map/pallas_call | solution.py:643
  170.9 1.3 slice.3
  172.2 0.0 copy-done
  172.2 0.0 copy-start.1
  172.2 1.0 copy.15
  173.2 0.0 copy-done.1
  173.2 0.0 copy-start.2
  173.2 0.6 copy.16
  173.8 0.1 copy-done.2
  173.9 0.6 copy.17
  (1 shorter events, 0.0 us)
Async XLA Ops:
  0.6 0.7 copy-start.4
  1.3 0.8 copy-start.3
  97.2 75.0 %copy-start = (bf16[32,16,1024]{2,1,0:T(8,128)(2,1)S(1)}, bf16[32,16,1024]{2,1,0:T(8,128)(2,1)}, u32[]{:S(2)}) copy-start(bf16[32,16,1024]{2,1,0:T(8,128)(2,1)} %get-tuple-element.22.pred) | copy-start | bytes 3145732
  172.2 1.0 copy-start.1
  173.2 0.7 copy-start.2

commit v2 on v1

v2 whole, which is shorter than its diff:
```python
import functools

import jax
import jax.numpy as jnp
from jax import lax
from jax.experimental import pallas as pl
from jax.experimental.pallas import tpu as pltpu
from jax.sharding import PartitionSpec as P

STEPS = 6
MEMBERS = 512
HALO = 6
EXT = 28
NC = 1024
HIGH = lax.Precision.HIGHEST
MESH = pl.DeviceIdType.MESH
F32 = jnp.float32
BF16 = jnp.bfloat16
VMEM_LIMIT = 56 * 1024 * 1024


def place():
    g = lax.axis_index("grid")
    m = lax.axis_index("member")
    return g, m


def plane_of(g, m):
    return (g // 16) * 8 + (m // 8) * 4 + (m // 2) % 4


def plane_peer(p, g, m):
    return (p // 8) * 16 + g % 16, ((p // 4) % 2) * 8 + (p % 4) * 2 + m % 2


def z_reducer(j):
    return (8 * j) // 3


def remote(src, dst, send, recv, where):
    return pltpu.make_async_remote_copy(
        src_ref=src, dst_ref=dst, send_sem=send, recv_sem=recv, device_id=where, device_id_type=MESH
    )


def signal(sem, where):
    pl.semaphore_signal(sem, inc=1, device_id=where, device_id_type=MESH)


def split3(value):
    a = value.astype(BF16)
    rest = value - a.astype(F32)
    b = rest.astype(BF16)
    c = (rest - b.astype(F32)).astype(BF16)
    return a, b, c


def across(value):
    return (value % 8) * 128 + value // 8


def fill_coefs(g, cce, dif, vel, coef):
    place_of = lax.broadcasted_iota(jnp.int32, (8, NC), 1)
    for quarter in range(4):
        rows = pl.ds(quarter * 8, 8)
        cls = cce[rows, :]
        d = jnp.zeros((8, NC), F32)
        vx = jnp.zeros((8, NC), F32)
        vy = jnp.zeros((8, NC), F32)
        for c in range(16):
            hit = cls == float(c)
            d = jnp.where(hit, dif[c], d)
            vx = jnp.where(hit, vel[0, c], vx)
            vy = jnp.where(hit, vel[1, c], vy)
        row = lax.broadcasted_iota(jnp.int32, (8, NC), 0) + (quarter * 8 - 8) + g * 16
        inside = jnp.logical_and(row >= 0, row < 512)
        values = (
            jnp.where(inside, 1.0 - 4.0 * d, 0.0),
            jnp.where(inside, d + 0.5 * vy, 0.0),
            jnp.where(inside, d - 0.5 * vy, 0.0),
            jnp.where(jnp.logical_and(inside, place_of > 0), d + 0.5 * vx, 0.0),
            jnp.where(jnp.logical_and(inside, place_of < NC - 1), d - 0.5 * vx, 0.0),
        )
        for i in range(5):
            for t in range(8):
                coef[t, quarter * 8:quarter * 8 + 8, i, :] = values[i][:, t * 128:(t + 1) * 128]


def inverse(a):
    lane = lax.broadcasted_iota(jnp.int32, (8, 128), 1)
    line = lax.broadcasted_iota(jnp.int32, (8, 128), 0)
    v = [a[8 * i:8 * i + 8] for i in range(16)]
    for t in range(16):
        col = [
            [jnp.broadcast_to(v[i][:, 8 * t + j:8 * t + j + 1], (8, 128)) for i in range(16)] for j in range(8)
        ]
        inside = jnp.logical_and(lane >= 8 * t, lane < 8 * t + 8)
        u = jnp.where(inside, (lane - 8 * t == line).astype(F32), v[t])
        k = [col[j][t] for j in range(8)]
        for s in range(8):
            inv = 1.0 / k[s][s:s + 1]
            here = line == s
            for j in range(s + 1, 8):
                r = k[j][s:s + 1] * inv
                k[j] = jnp.where(here, r, k[j] - k[s] * r)
            r = u[s:s + 1] * inv
            u = jnp.where(here, r, u - k[s] * r)
        rows = [jnp.broadcast_to(u[s:s + 1], (8, 128)) for s in range(8)]
        for d in range(1, 16):
            i = (t + d) % 16
            w = jnp.where(inside, 0.0, v[i])
            x0 = col[0][i] * rows[0] + col[1][i] * rows[1]
            x1 = col[2][i] * rows[2] + col[3][i] * rows[3]
            x2 = col[4][i] * rows[4] + col[5][i] * rows[5]
            x3 = col[6][i] * rows[6] + col[7][i] * rows[7]
            v[i] = w - ((x0 + x1) + (x2 + x3))
        v[t] = u
    return jnp.concatenate(v, axis=0)


def mm(a, b):
    return jnp.dot(a, b, precision=HIGH, preferred_element_type=F32)


def solve(ff, asc, wsc, xcol):
    row = lax.broadcasted_iota(jnp.int32, (128, 128), 0)
    col = lax.broadcasted_iota(jnp.int32, (128, 128), 1)
    ridge = jnp.where(row == col, float(MEMBERS - 1), 0.0)

    def tile(h, t):
        return ff[h, :, t].reshape(128, 128)

    def right(h, first):
        keep = jnp.logical_and(col >= first, col < first + 3)
        part = jnp.sum(jnp.where(keep, tile(h, 5), 0.0), axis=1, keepdims=True)
        return jnp.broadcast_to(part, (128, 128))

    asc[...] = jnp.zeros_like(asc)
    where = {
        (0, 0): (0, 0), (0, 1): (0, 1), (0, 2): (0, 2), (0, 3): (0, 3), (3, 3): (0, 4),
        (1, 1): (1, 0), (1, 2): (1, 1), (1, 3): (1, 2), (2, 2): (1, 3), (2, 3): (1, 4),
    }
    for (i, j), (h, t) in where.items():
        block = tile(h, t)
        asc[i, :, 128 * j:128 * j + 128] = block + ridge if i == j else block
    for i, (h, first) in enumerate(((0, 0), (1, 0), (1, 64), (0, 64))):
        asc[i, :, 512:640] = right(h, first)

    def eliminate(k, carry):
        mine = pl.ds(pl.multiple_of(k * 128, 128), 128)
        w = mm(inverse(asc[k, :, mine]), asc[k])
        wsc[k] = w

        def update(i, carry):
            other = asc[k, :, pl.ds(pl.multiple_of(i * 128, 128), 128)].T
            asc[i] = asc[i] - mm(other, w)
            return carry

        lax.fori_loop(k + 1, 4, update, 0)
        return carry

    lax.fori_loop(0, 4, eliminate, 0)
    xcol[...] = jnp.zeros_like(xcol)

    def back(i, carry):
        k = 3 - i
        xcol[pl.ds(pl.multiple_of(k * 128, 128), 128), :] = wsc[k, :, 512:640] - mm(wsc[k, :, 0:512], xcol[...])
        return carry

    lax.fori_loop(0, 4, back, 0)


def kernel(
    x_ref, cc_ref, dif, vel, cells, count, value_ref, scale_ref, pred, mean_out, obs_out, mix_out,
    turn, a_buf, b_buf, coef, perm, onehot, pbf, clsf, cce, hsend, hrecv, wv, wrecv, sbuf, samples,
    fpart, rcore, rplane, zsend, zrecv, fin, ff, asc, wsc, xcol, fields, tall, line,
    s_halo, r_halo, s_cls, r_cls, s_w, r_w, s_s, r_s, s_c, r_c, s_p, r_p, s_z, r_z, s_g, r_g, s_a, r_a, s_b, r_b,
    s_f, r_f, s_o, r_o, s_l, r_l, relay,
):
    g, m = place()
    z, xl = g % 16, g // 16
    core = m % 2
    p = plane_of(g, m)
    other = m + 1 - 2 * core
    sender = g // 2 == m
    crossing = jnp.logical_or(g == 15, g == 16)
    barrier = pltpu.get_barrier_semaphore()

    def z_peer(d):
        return xl * 16 + (z + d) % 16, m

    signal(barrier, z_peer(1))
    signal(barrier, z_peer(15))

    @pl.when(crossing)
    def _():
        signal(barrier, (31 - g, m))

    def greet(d, carry):
        signal(barrier, (g, (m + d) % 16))
        signal(barrier, plane_peer((p + d) % 16, g, m))
        return carry

    lax.fori_loop(1, 16, greet, 0)

    at_row = lax.broadcasted_iota(jnp.int32, (NC, 128), 0)
    at_col = lax.broadcasted_iota(jnp.int32, (NC, 128), 1)
    for t in range(8):
        perm[:, t * 128:(t + 1) * 128] = (at_row == at_col * 8 + t).astype(F32).astype(BF16)
    both = jnp.concatenate([x_ref[...].reshape(512, NC), cc_ref[...].astype(F32).astype(BF16)], axis=0)
    for t in range(8):
        moved = jnp.dot(both, perm[:, t * 128:(t + 1) * 128], preferred_element_type=F32)
        turn[t] = moved[0:512]
        clsf[:, t * 128:(t + 1) * 128] = moved[512:528]

    def shuffle(r, carry):
        for q in range(4):
            for t in range(8):
                a_buf[q, r + HALO, :, t * 128:(t + 1) * 128] = turn[t, pl.ds(q * 128 + r, 8, stride=16), :]
        return carry

    lax.fori_loop(0, 16, shuffle, 0)
    for side in range(2):
        def pack(r, carry, side=side):
            for h in range(2):
                pair = [a_buf[2 * h + i, r + HALO + side * 10] for i in range(2)]
                hsend[side, h, r] = jnp.concatenate(pair, axis=0).astype(BF16)
            return carry

        lax.fori_loop(0, HALO, pack, 0)

    pl.semaphore_wait(barrier, 32 + crossing.astype(jnp.int32))

    def up(h):
        return remote(hsend.at[0, h], hrecv.at[1, h], s_halo.at[0, h], r_halo.at[1, h], (g - 1, m))

    def down(h):
        return remote(hsend.at[1, h], hrecv.at[0, h], s_halo.at[1, h], r_halo.at[0, h], (g + 1, m))

    cup = remote(clsf.at[pl.ds(0, 8)], cce.at[pl.ds(24, 8)], s_cls.at[0], r_cls.at[1], (g - 1, m))
    cdown = remote(clsf.at[pl.ds(8, 8)], cce.at[pl.ds(0, 8)], s_cls.at[1], r_cls.at[0], (g + 1, m))

    @pl.when(g > 0)
    def _():
        cup.start()
        up(0).start()
        up(1).start()

    @pl.when(g < 31)
    def _():
        cdown.start()
        down(0).start()
        down(1).start()

    def tell(k):
        signal(relay.at[k], z_peer(2**k))
        signal(relay.at[k], z_peer(16 - 2**k))

    tell(0)
    cce[pl.ds(8, 16), :] = clsf[...]

    @pl.when(g == 0)
    def _():
        hrecv[0] = jnp.zeros((2, HALO, 16, NC), BF16)
        cce[pl.ds(0, 8), :] = jnp.zeros((8, NC), F32)

    @pl.when(g == 31)
    def _():
        hrecv[1] = jnp.zeros((2, HALO, 16, NC), BF16)
        cce[pl.ds(24, 8), :] = jnp.zeros((8, NC), F32)

    slot = lax.broadcasted_iota(jnp.int32, (1, 128), 1)
    for s in range(32):
        valid = (slot < count[0, s]).astype(F32)
        wv[s] = jnp.concatenate([scale_ref[0, s:s + 1, :] * valid, value_ref[0, s:s + 1, :]], axis=1)
    at_place = lax.broadcasted_iota(jnp.int32, (NC, 128), 0)

    def mark(o, carry):
        spot = across(cells[0, pl.ds(o, 1), :] % NC)
        onehot[o] = (at_place == spot).astype(F32).astype(BF16)
        return carry

    lax.fori_loop(0, 32, mark, 0)
    pl.semaphore_wait(relay.at[0], 2)
    tell(1)

    @pl.when(g > 0)
    def _():
        cup.wait_send()
        cdown.wait_recv()

    @pl.when(g < 31)
    def _():
        cdown.wait_send()
        cup.wait_recv()

    fill_coefs(g, cce, dif, vel, coef)
    bufs = (a_buf, b_buf)

    def edge(src, q, r):
        return pltpu.roll(src[q, r, :, 7 * 128:], 1, 1), pltpu.roll(src[q, r, :, :128], 127, 1)

    for h in range(2):
        @pl.when(g > 0)
        def _(h=h):
            up(h).wait_send()
            down(h).wait_recv()

        @pl.when(g < 31)
        def _(h=h):
            down(h).wait_send()
            up(h).wait_recv()

        if h == 1:
            pl.semaphore_wait(relay.at[1], 2)
            tell(2)
        for side in range(2):
            def widen(r, carry, side=side, h=h):
                rows = hrecv[side, h, r].astype(F32)
                a_buf[2 * h, r + side * 22] = rows[0:8]
                a_buf[2 * h + 1, r + side * 22] = rows[8:16]
                return carry

            lax.fori_loop(0, HALO, widen, 0)
        for k in range(STEPS):
            src, dst = bufs[k % 2], bufs[(k + 1) % 2]

            def advance(r, carry, src=src, dst=dst, k=k, h=h):
                pair = []
                for q in (2 * h, 2 * h + 1):
                    mid = [src[q, r, :, t * 128:(t + 1) * 128] for t in range(8)]
                    first, last = edge(src, q, r)
                    tiles = []
                    for t in range(8):
                        lanes = slice(t * 128, (t + 1) * 128)
                        c = [jnp.broadcast_to(coef[t, r + 2, i:i + 1, :], (8, 128)) for i in range(5)]
                        left = mid[t - 1] if t else first
                        right = mid[t + 1] if t < 7 else last
                        out = c[0] * mid[t]
                        out = out + c[1] * src[q, r - 1, :, lanes] + c[2] * src[q, r + 1, :, lanes]
                        out = out + c[3] * left + c[4] * right
                        if k < STEPS - 1:
                            dst[q, r, :, lanes] = out
                        tiles.append(out)
                    pair.append(jnp.concatenate(tiles, axis=1))
                if k == STEPS - 1:
                    pbf[pl.ds((r - HALO) * 32 + 16 * h, 16), :] = jnp.concatenate(pair, axis=0).astype(BF16)
                return carry

            lax.fori_loop(k + 1, EXT - 1 - k, advance, 0, unroll=4)

    def sample(chunk):
        row = jnp.concatenate([cells[0, pl.ds(2 * chunk + i, 1), :] for i in range(2)], axis=1) // NC
        wide = jnp.dot(
            pbf[...], jnp.concatenate([onehot[2 * chunk], onehot[2 * chunk + 1]], axis=1), preferred_element_type=F32
        )
        total = jnp.zeros((32, 256), F32)
        for r in range(16):
            total = total + jnp.where(row == r, wide[r * 32:(r + 1) * 32], 0.0)
        return total.astype(BF16)

    def scatter(d, carry):
        peer = (m + d) % 16
        sbuf[d] = sample(peer)
        remote(sbuf.at[d], samples.at[m], s_s.at[d], r_s.at[m], (g, peer)).start()
        return carry

    lax.fori_loop(1, 16, scatter, 0)
    samples[m] = sample(m)

    pl.semaphore_wait(relay.at[2], 2)
    signal(relay.at[3], (g + 16 - 32 * xl, m))
    pl.semaphore_wait(relay.at[3], 1)

    @pl.when(sender)
    def _():
        def give(d, carry):
            s = (g + d) % 32
            remote(wv.at[s], wrecv.at[g % 2], s_w.at[d], r_w.at[g % 2], (s, m)).start()
            return carry

        lax.fori_loop(1, 32, give, 0)
        wrecv[g % 2] = wv[g]

    def scattered(d, carry):
        peer = (m + d) % 16
        c = remote(sbuf.at[d], samples.at[peer], s_s.at[d], r_s.at[peer], (g, peer))
        c.wait_send()
        c.wait_recv()
        return carry

    lax.fori_loop(1, 16, scattered, 0)

    @pl.when(sender)
    def _():
        def given(d, carry):
            remote(wv.at[g], wrecv.at[g % 2], s_w.at[d], r_w.at[g % 2], (g, m)).wait_send()
            return carry

        lax.fori_loop(1, 32, given, 0)

    for o in range(2):
        @pl.when(2 * m + o != g)
        def _(o=o):
            remote(wv.at[g], wrecv.at[o], s_w.at[0], r_w.at[o], (g, m)).wait_recv()

    sampled = samples[...].reshape(MEMBERS, 256).astype(F32)
    mean = jnp.sum(sampled, axis=0, keepdims=True) / MEMBERS
    weight = jnp.concatenate([wrecv[0, :, 0:128], wrecv[1, :, 0:128]], axis=1)
    value = jnp.concatenate([wrecv[0, :, 128:256], wrecv[1, :, 128:256]], axis=1)
    panel = ((sampled - mean) * weight).astype(BF16)
    parts = split3((value - mean) * weight)
    line_at = lax.broadcasted_iota(jnp.int32, (128, 256), 0)
    dep_one = jnp.zeros((128, 256), F32)
    dep_two = jnp.zeros((128, 256), F32)
    for i in range(3):
        dep_one = jnp.where(line_at == i, parts[i].astype(F32), dep_one)
        dep_two = jnp.where(line_at == 64 + i, parts[i].astype(F32), dep_two)
    dep_one = dep_one.astype(BF16)
    dep_two = dep_two.astype(BF16)
    blk = [panel[i * 128:(i + 1) * 128] for i in range(4)]

    def outer(a, b):
        return lax.dot_general(a, b, (((1,), (1,)), ((), ())), preferred_element_type=F32)

    pairs = (
        ((0, 0), (0, 1), (0, 2), (0, 3), (3, 3)),
        ((1, 1), (1, 2), (1, 3), (2, 2), (2, 3)),
    )
    for h in range(2):
        for t in range(5):
            i, j = pairs[h][t]
            fpart[h, :, t] = outer(blk[i], blk[j]).reshape(16, 8, 128)
        fpart[h, :, 5] = (outer(blk[h], dep_one) + outer(blk[3 - h], dep_two)).reshape(16, 8, 128)

    swap = remote(fpart.at[1 - core], rcore, s_c.at[0], r_c.at[0], (g, other))
    swap.start()
    swap.wait()

    def pair_sum(i, carry):
        rcore[i] = rcore[i] + fpart[core, i]
        return carry

    lax.fori_loop(0, 16, pair_sum, 0)

    def plane_give(d, carry):
        q = (p + d) % 16
        remote(rcore.at[q], rplane.at[p], s_p.at[d], r_p.at[p], plane_peer(q, g, m)).start()
        return carry

    lax.fori_loop(1, 16, plane_give, 0)

    for t in range(8):
        back = lax.dot_general(
            pbf[...], perm[t * 128:(t + 1) * 128, :], (((1,), (1,)), ((), ())), preferred_element_type=F32
        )
        for r in range(16):
            for q in range(4):
                at = r * 32 + q * 8
                turn[t, pl.ds(q * 128 + r, 8, stride=16), :] = back[at:at + 8]

    def finish(i, carry):
        for t in range(8):
            pred[i, :, t * 128:(t + 1) * 128] = turn[t, pl.ds(i * 16, 16), :].astype(BF16)
        return carry

    lax.fori_loop(0, 32, finish, 0)

    def plane_take(d, total):
        q = (p + d) % 16
        remote(rcore.at[q], rplane.at[q], s_p.at[d], r_p.at[q], plane_peer(q, g, m)).wait_recv()
        return total + rplane[q]

    zsend[...] = lax.fori_loop(1, 16, plane_take, rcore[p])

    for j in range(6):
        @pl.when(z != z_reducer(j))
        def _(j=j):
            remote(zsend.at[j], zrecv.at[z], s_z.at[j], r_z.at[z], (xl * 16 + z_reducer(j), m)).start()

    for j in range(6):
        @pl.when(z == z_reducer(j))
        def _(j=j):
            def z_take(d, total):
                q = (z + d) % 16
                remote(zsend.at[j], zrecv.at[q], s_z.at[j], r_z.at[q], (xl * 16 + q, m)).wait_recv()
                return total + zrecv[q]

            fin[p, j] = lax.fori_loop(1, 16, z_take, zsend[j])

            def z_give(d, carry):
                q = (z + d) % 16
                remote(fin.at[p, j], fin.at[p, j], s_g.at[d], r_g.at[j], (xl * 16 + q, m)).start()
                return carry

            lax.fori_loop(1, 16, z_give, 0)

    for j in range(6):
        @pl.when(z != z_reducer(j))
        def _(j=j):
            remote(fin.at[p, j], fin.at[p, j], s_g.at[0], r_g.at[j], (xl * 16 + z_reducer(j), m)).wait_recv()

    def plane_send(d, carry):
        q = (p + d) % 16
        remote(fin.at[p], fin.at[p], s_a.at[d], r_a.at[p], plane_peer(q, g, m)).start()
        return carry

    lax.fori_loop(1, 16, plane_send, 0)

    def plane_got(d, carry):
        q = (p + d) % 16
        remote(fin.at[q], fin.at[q], s_a.at[d], r_a.at[q], plane_peer(q, g, m)).wait_recv()
        return carry

    lax.fori_loop(1, 16, plane_got, 0)
    home = remote(fin, ff.at[core], s_b.at[0], r_b.at[0], (g, other))
    home.start()

    def keep(i, carry):
        ff[core, i] = fin[i]
        return carry

    lax.fori_loop(0, 16, keep, 0)
    home.wait()

    def field_give(d, carry):
        q = (m + d) % 16
        mine = pbf.at[pl.ds(pl.multiple_of(q * 32, 32), 32)]
        remote(mine, fields.at[m], s_f.at[d], r_f.at[m], (g, q)).start()
        return carry

    lax.fori_loop(1, 16, field_give, 0)
    fields[m] = pbf[pl.ds(pl.multiple_of(m * 32, 32), 32), :]
    for i in range(2):
        lanes = slice(i * 128, (i + 1) * 128)

        @pl.when(2 * m + i != g)
        def _(i=i, lanes=lanes):
            src = samples.at[:, :, lanes]
            remote(src, tall.at[g % 2], s_o.at[i], r_o.at[g % 2], (2 * m + i, g // 2)).start()

        @pl.when(2 * m + i == g)
        def _(i=i, lanes=lanes):
            tall[g % 2] = samples[:, :, lanes]

    solve(ff, asc, wsc, xcol)

    x = xcol[...]
    shift = 1.0 / MEMBERS - jnp.sum(x[:, 0:1], axis=0, keepdims=True) / MEMBERS
    coefs = []
    for k in range(4):
        piece = x[k * 128:(k + 1) * 128].T[0:8, :]
        mix_out[:, k * 128:(k + 1) * 128] = piece
        coefs.append(piece + shift)
    pieces = split3(jnp.concatenate(coefs, axis=1))

    def weigh(array):
        total = jnp.zeros((8, array.shape[1]), F32)
        for piece in pieces:
            total = total + jnp.dot(piece, array, preferred_element_type=F32)
        return total[0:1]

    def field_take(d, carry):
        q = (m + d) % 16
        mine = pbf.at[pl.ds(pl.multiple_of(q * 32, 32), 32)]
        c = remote(mine, fields.at[q], s_f.at[d], r_f.at[q], (g, q))
        c.wait_send()
        c.wait_recv()
        return carry

    lax.fori_loop(1, 16, field_take, 0)
    for i in range(2):
        @pl.when(2 * m + i != g)
        def _(i=i):
            src = samples.at[:, :, slice(0, 128)]
            remote(src, tall.at[i], s_o.at[i], r_o.at[i], (2 * m + i, g // 2)).wait_recv()
            remote(src, tall.at[i], s_o.at[i], r_o.at[i], (2 * m + i, g // 2)).wait_send()

    parts = [weigh(fields[...].reshape(MEMBERS, NC))]
    parts += [weigh(tall[i].reshape(MEMBERS, 128)) for i in range(2)]
    line[m] = jnp.concatenate(parts, axis=1)

    def line_give(d, carry):
        q = (m + d) % 16
        remote(line.at[m], line.at[m], s_l.at[d], r_l.at[m], (g, q)).start()
        return carry

    lax.fori_loop(1, 16, line_give, 0)

    def drain(d, carry):
        q = (p + d) % 16
        remote(rcore.at[q], rplane.at[q], s_p.at[d], r_p.at[q], plane_peer(q, g, m)).wait_send()
        remote(fin.at[p], fin.at[p], s_a.at[d], r_a.at[p], plane_peer(q, g, m)).wait_send()
        return carry

    lax.fori_loop(1, 16, drain, 0)
    for j in range(6):
        @pl.when(z != z_reducer(j))
        def _(j=j):
            remote(zsend.at[j], zrecv.at[z], s_z.at[j], r_z.at[z], (xl * 16 + z_reducer(j), m)).wait_send()

        @pl.when(z == z_reducer(j))
        def _(j=j):
            def z_given(d, carry):
                q = (z + d) % 16
                remote(fin.at[p, j], fin.at[p, j], s_g.at[d], r_g.at[j], (xl * 16 + q, m)).wait_send()
                return carry

            lax.fori_loop(1, 16, z_given, 0)

    def line_take(d, carry):
        q = (m + d) % 16
        c = remote(line.at[m], line.at[q], s_l.at[d], r_l.at[q], (g, q))
        c.wait_send()
        c.wait_recv()
        return carry

    lax.fori_loop(1, 16, line_take, 0)

    rows = jnp.concatenate([line[r][:, 0:NC] for r in range(16)], axis=0)
    total = jnp.zeros((16, NC), F32)
    for piece in split3(rows):
        total = total + lax.dot_general(piece, perm[...], (((1,), (1,)), ((), ())), preferred_element_type=F32)
    mean_out[...] = total
    for s in range(32):
        first = NC + (s % 2) * 128
        obs_out[s:s + 1, :] = line[s // 2][:, first:first + 128]


def local(
    prior_sample_matrix, cell_class, diffusion_table, velocity_table, obs_cells, obs_count, obs_value, obs_scale
):
    vmem = pl.BlockSpec(memory_space=pltpu.VMEM)
    smem = pl.BlockSpec(memory_space=pltpu.SMEM)
    dma = pltpu.SemaphoreType.DMA
    pred, mean, obs, mix = pl.pallas_call(
        kernel,
        out_shape=(
            jax.ShapeDtypeStruct((32, 16, NC), BF16),
            jax.ShapeDtypeStruct((16, NC), F32),
            jax.ShapeDtypeStruct((32, 128), F32),
            jax.ShapeDtypeStruct((8, MEMBERS), F32),
        ),
        in_specs=[vmem, vmem, smem, smem, vmem, smem, vmem, vmem],
        out_specs=(vmem, vmem, vmem, vmem),
        scratch_shapes=[
            pltpu.VMEM((8, 512, 128), F32),
            pltpu.VMEM((4, EXT, 8, NC), F32),
            pltpu.VMEM((4, EXT, 8, NC), F32),
            pltpu.VMEM((8, 32, 8, 128), F32),
            pltpu.VMEM((NC, NC), BF16),
            pltpu.VMEM((32, NC, 128), BF16),
            pltpu.VMEM((512, NC), BF16),
            pltpu.VMEM((16, NC), F32),
            pltpu.VMEM((32, NC), F32),
            pltpu.VMEM((2, 2, HALO, 16, NC), BF16),
            pltpu.VMEM((2, 2, HALO, 16, NC), BF16),
            pltpu.VMEM((32, 1, 256), F32),
            pltpu.VMEM((2, 1, 256), F32),
            pltpu.VMEM((16, 32, 256), BF16),
            pltpu.VMEM((16, 32, 256), BF16),
            pltpu.VMEM((2, 16, 6, 8, 128), F32),
            pltpu.VMEM((16, 6, 8, 128), F32),
            pltpu.VMEM((16, 6, 8, 128), F32),
            pltpu.VMEM((6, 8, 128), F32),
            pltpu.VMEM((16, 8, 128), F32),
            pltpu.VMEM((16, 6, 8, 128), F32),
            pltpu.VMEM((2, 16, 6, 8, 128), F32),
            pltpu.VMEM((4, 128, 640), F32),
            pltpu.VMEM((4, 128, 640), F32),
            pltpu.VMEM((MEMBERS, 128), F32),
            pltpu.VMEM((16, 32, NC), BF16),
            pltpu.VMEM((2, 16, 32, 128), BF16),
            pltpu.VMEM((16, 1, NC + 256), F32),
            dma((2, 2)), dma((2, 2)), dma((2,)), dma((2,)), dma((32,)), dma((2,)), dma((16,)), dma((16,)),
            dma((1,)), dma((1,)), dma((16,)), dma((16,)), dma((6,)), dma((16,)), dma((16,)), dma((6,)),
            dma((16,)), dma((16,)), dma((1,)), dma((1,)),
            dma((16,)), dma((16,)), dma((2,)), dma((2,)), dma((16,)), dma((16,)),
            pltpu.SemaphoreType.REGULAR((4,)),
        ],
        compiler_params=pltpu.CompilerParams(
            collective_id=0, has_side_effects=True, vmem_limit_bytes=VMEM_LIMIT
        ),
    )(prior_sample_matrix, cell_class, diffusion_table, velocity_table, obs_cells, obs_count, obs_value, obs_scale)
    return pred, mean, obs.reshape(1, 32, 128), mix[0]


def solution(mesh):
    in_specs = (
        P("member", "grid", None),
        P("grid", None),
        P(),
        P(),
        P("grid", None, None),
        P("grid", None),
        P("grid", None, None),
        P("grid", None, None),
    )
    out_specs = (P("member", "grid", None), P("grid", None), P("grid", None, None), P())
    return jax.shard_map(local, mesh=mesh, in_specs=in_specs, out_specs=out_specs, check_vma=False)
```

time: 175 us -> 137 us (0.78)
  Pallas kernels: 168 us -> 130 us
    pallas_call x3 -> x1, Pallas kernels: 168 us -> 130 us  [local(): pl.pallas_call(kernel, out_shape=(jax.ShapeDtypeStruct((32, 16, NC), BF16...]
    unnamed x13 -> x7, local copies, waits for them, and re-layouts: 2.95 us -> 3.66 us
where the time goes in v2:
time: 137 us; the launch traced here: 136 us
  Pallas kernels  130 us (95%)
  local copies, waits for them, and re-layouts  4.96 us (4%)
    pallas_call x1, Pallas kernels, local(): pl.pallas_call(kernel, out_shape=(jax.ShapeDtypeStruct((32, 16, NC), BF16...  130 us
    unnamed x7, local copies, waits for them, and re-layouts  3.66 us

profile of v2, /device:TPU:1, one launch (start us, length us, event | category | flops | bytes accessed | tf_op | source)
XLA Modules:
  0.0 135.9 jit_solution(15251704358477031716)
XLA Ops:
  0.6 130.3 %shard_map.111 = (bf16[32,16,1024]{2,1,0:T(8,128)(2,1)}, f32[16,1024]{1,0:T(8,128)}, f32[32,128]{1,0:T(8,128)}, f32[8,512]{1,0:T(8,128)}) custom-call(bf16[32,16,1024]{2,1,0:T(8,128)(2,1)} %x_ref.1, s32[16,1024]{1,0:T(8,128)} %cc_ref.1, f32[16]{0:T(128)} %dif.1, f32[2,16]{1,0:T(2,128)} %vel.1, s32[1,32,128]{2,1,0:T(8,128)} %cells.1, s32[1,32]{1,0:T(1,128)} %count.1, ...), custom_call_target="tpu_custom_call" | custom-call | tf_op jit(solution)/shard_map/pallas_call | solution.py:636
  130.9 1.3 slice.3
  132.2 0.0 copy-start
  132.2 2.3 %copy.15 = bf16[32,16,1024]{2,1,0:T(8,128)(2,1)} copy(bf16[32,16,1024]{2,1,0:T(8,128)(2,1)} %get-tuple-element.16) | data formatting | bytes 2097152
  134.5 0.0 copy-done
  134.5 0.0 copy-start.1
  134.5 0.6 copy.16
  135.2 0.1 copy-done.1
  135.3 0.6 copy.17
Async XLA Ops:
  132.2 2.3 %copy-start = (f32[16,1024]{1,0:T(8,128)S(1)}, f32[16,1024]{1,0:T(8,128)}, u32[]{:S(2)}) copy-start(f32[16,1024]{1,0:T(8,128)} %get-tuple-element.17) | copy-start | bytes 196612
  134.5 0.7 copy-start.1

commit v3 on v2

--- a/solution.py
+++ b/solution.py
@@ -90,13 +90,14 @@
     lane = lax.broadcasted_iota(jnp.int32, (8, 128), 1)
     line = lax.broadcasted_iota(jnp.int32, (8, 128), 0)
     v = [a[8 * i:8 * i + 8] for i in range(16)]
+
+    def column(i, t, j):
+        return jnp.broadcast_to(v[i][:, 8 * t + j:8 * t + j + 1], (8, 128))
+
     for t in range(16):
-        col = [
-            [jnp.broadcast_to(v[i][:, 8 * t + j:8 * t + j + 1], (8, 128)) for i in range(16)] for j in range(8)
-        ]
         inside = jnp.logical_and(lane >= 8 * t, lane < 8 * t + 8)
         u = jnp.where(inside, (lane - 8 * t == line).astype(F32), v[t])
-        k = [col[j][t] for j in range(8)]
+        k = [column(t, t, j) for j in range(8)]
         for s in range(8):
             inv = 1.0 / k[s][s:s + 1]
             here = line == s
@@ -105,9 +106,10 @@
                 k[j] = jnp.where(here, r, k[j] - k[s] * r)
             r = u[s:s + 1] * inv
             u = jnp.where(here, r, u - k[s] * r)
+        others = [(t + d) % 16 for d in range(1, 16)]
+        col = [{i: column(i, t, j) for i in others} for j in range(8)]
         rows = [jnp.broadcast_to(u[s:s + 1], (8, 128)) for s in range(8)]
-        for d in range(1, 16):
-            i = (t + d) % 16
+        for i in others:
             w = jnp.where(inside, 0.0, v[i])
             x0 = col[0][i] * rows[0] + col[1][i] * rows[1]
             x1 = col[2][i] * rows[2] + col[3][i] * rows[3]
@@ -122,7 +124,7 @@
     return jnp.dot(a, b, precision=HIGH, preferred_element_type=F32)
 
 
-def solve(ff, asc, wsc, xcol):
+def solve(ff, asc, wsc, inv, xcol):
     row = lax.broadcasted_iota(jnp.int32, (128, 128), 0)
     col = lax.broadcasted_iota(jnp.int32, (128, 128), 1)
     ridge = jnp.where(row == col, float(MEMBERS - 1), 0.0)
@@ -135,7 +137,6 @@
         part = jnp.sum(jnp.where(keep, tile(h, 5), 0.0), axis=1, keepdims=True)
         return jnp.broadcast_to(part, (128, 128))
 
-    asc[...] = jnp.zeros_like(asc)
     where = {
         (0, 0): (0, 0), (0, 1): (0, 1), (0, 2): (0, 2), (0, 3): (0, 3), (3, 3): (0, 4),
         (1, 1): (1, 0), (1, 2): (1, 1), (1, 3): (1, 2), (2, 2): (1, 3), (2, 3): (1, 4),
@@ -147,33 +148,30 @@
         asc[i, :, 512:640] = right(h, first)
 
     def eliminate(k, carry):
-        mine = pl.ds(pl.multiple_of(k * 128, 128), 128)
-        w = mm(inverse(asc[k, :, mine]), asc[k])
-        wsc[k] = w
-
-        def update(i, carry):
-            other = asc[k, :, pl.ds(pl.multiple_of(i * 128, 128), 128)].T
-            asc[i] = asc[i] - mm(other, w)
-            return carry
-
-        lax.fori_loop(k + 1, 4, update, 0)
+        inv[...] = inverse(asc[k, :, pl.ds(pl.multiple_of(k * 128, 128), 128)])
+        for n in range(4):
+            @pl.when(k == n)
+            def _(n=n):
+                w = mm(inv[...], asc[n, :, 128 * n + 128:640])
+                wsc[n, :, 128 * n + 128:640] = w
+                for i in range(n + 1, 4):
+                    other = asc[n, :, 128 * i:128 * i + 128].T
+                    asc[i, :, 128 * i:640] = asc[i, :, 128 * i:640] - mm(other, w[:, 128 * (i - n - 1):])
         return carry
 
     lax.fori_loop(0, 4, eliminate, 0)
-    xcol[...] = jnp.zeros_like(xcol)
-
-    def back(i, carry):
-        k = 3 - i
-        xcol[pl.ds(pl.multiple_of(k * 128, 128), 128), :] = wsc[k, :, 512:640] - mm(wsc[k, :, 0:512], xcol[...])
-        return carry
-
-    lax.fori_loop(0, 4, back, 0)
+    for k in reversed(range(4)):
+        y = wsc[k, :, 512:640]
+        if k < 3:
+            y = y - mm(wsc[k, :, 128 * k + 128:512], xcol[128 * k + 128:512, :])
+        xcol[128 * k:128 * k + 128, :] = y
 
 
 def kernel(
-    x_ref, cc_ref, dif, vel, cells, count, value_ref, scale_ref, pred, mean_out, obs_out, mix_out,
+    x_hbm, cc_hbm, dif, vel, cells_hbm, count, value_hbm, scale_hbm, pred_hbm, mean_hbm, obs_hbm, mix_hbm,
+    x_ref, cc_ref, cells, value_ref, scale_ref, pred, mean_out, obs_out, mix_out, s_in, s_out,
     turn, a_buf, b_buf, coef, perm, onehot, pbf, clsf, cce, hsend, hrecv, wv, wrecv, sbuf, samples,
-    fpart, rcore, rplane, zsend, zrecv, fin, ff, asc, wsc, xcol, fields, tall, line,
+    fpart, rcore, rplane, zsend, zrecv, fin, ff, asc, wsc, inv, xcol, fields, osend, orecv, line,
     s_halo, r_halo, s_cls, r_cls, s_w, r_w, s_s, r_s, s_c, r_c, s_p, r_p, s_z, r_z, s_g, r_g, s_a, r_a, s_b, r_b,
     s_f, r_f, s_o, r_o, s_l, r_l, relay,
 ):
@@ -189,6 +187,13 @@
     def z_peer(d):
         return xl * 16 + (z + d) % 16, m
 
+    arrays = ((x_hbm, x_ref), (cc_hbm, cc_ref), (cells_hbm, cells), (value_hbm, value_ref), (scale_hbm, scale_ref))
+    loads = [pltpu.make_async_copy(a, b, s_in.at[i]) for i, (a, b) in enumerate(arrays)]
+    for load in loads:
+        load.start()
+    arrays = ((pred, pred_hbm), (mean_out, mean_hbm), (obs_out, obs_hbm), (mix_out, mix_hbm))
+    stores = [pltpu.make_async_copy(a, b, s_out.at[i]) for i, (a, b) in enumerate(arrays)]
+
     signal(barrier, z_peer(1))
     signal(barrier, z_peer(15))
 
@@ -207,6 +212,8 @@
     at_col = lax.broadcasted_iota(jnp.int32, (NC, 128), 1)
     for t in range(8):
         perm[:, t * 128:(t + 1) * 128] = (at_row == at_col * 8 + t).astype(F32).astype(BF16)
+    loads[0].wait()
+    loads[1].wait()
     both = jnp.concatenate([x_ref[...].reshape(512, NC), cc_ref[...].astype(F32).astype(BF16)], axis=0)
     for t in range(8):
         moved = jnp.dot(both, perm[:, t * 128:(t + 1) * 128], preferred_element_type=F32)
@@ -244,13 +251,11 @@
     def _():
         cup.start()
         up(0).start()
-        up(1).start()
 
     @pl.when(g < 31)
     def _():
         cdown.start()
         down(0).start()
-        down(1).start()
 
     def tell(k):
         signal(relay.at[k], z_peer(2**k))
@@ -269,6 +274,8 @@
         hrecv[1] = jnp.zeros((2, HALO, 16, NC), BF16)
         cce[pl.ds(24, 8), :] = jnp.zeros((8, NC), F32)
 
+    for load in loads[2:]:
+        load.wait()
     slot = lax.broadcasted_iota(jnp.int32, (1, 128), 1)
     for s in range(32):
         valid = (slot < count[0, s]).astype(F32)
@@ -281,24 +288,38 @@
         return carry
 
     lax.fori_loop(0, 32, mark, 0)
+
+    @pl.when(g > 0)
+    def _():
+        up(1).start()
+        cup.wait_send()
+        cdown.wait_recv()
+
+    @pl.when(g < 31)
+    def _():
+        down(1).start()
+        cdown.wait_send()
+        cup.wait_recv()
+
     pl.semaphore_wait(relay.at[0], 2)
     tell(1)
 
-    @pl.when(g > 0)
-    def _():
-        cup.wait_send()
-        cdown.wait_recv()
-
-    @pl.when(g < 31)
-    def _():
-        cdown.wait_send()
-        cup.wait_recv()
-
     fill_coefs(g, cce, dif, vel, coef)
     bufs = (a_buf, b_buf)
 
     def edge(src, q, r):
         return pltpu.roll(src[q, r, :, 7 * 128:], 1, 1), pltpu.roll(src[q, r, :, :128], 127, 1)
+
+    def give_weights():
+        @pl.when(sender)
+        def _():
+            def give(d, carry):
+                s = (g + d) % 32
+                remote(wv.at[s], wrecv.at[g % 2], s_w.at[d], r_w.at[g % 2], (s, m)).start()
+                return carry
+
+            lax.fori_loop(1, 32, give, 0)
+            wrecv[g % 2] = wv[g]
 
     for h in range(2):
         @pl.when(g > 0)
@@ -311,9 +332,6 @@
             down(h).wait_send()
             up(h).wait_recv()
 
-        if h == 1:
-            pl.semaphore_wait(relay.at[1], 2)
-            tell(2)
         for side in range(2):
             def widen(r, carry, side=side, h=h):
                 rows = hrecv[side, h, r].astype(F32)
@@ -348,6 +366,15 @@
                 return carry
 
             lax.fori_loop(k + 1, EXT - 1 - k, advance, 0, unroll=4)
+            if (h, k) == (0, 0):
+                pl.semaphore_wait(relay.at[1], 2)
+                tell(2)
+            if (h, k) == (0, 4):
+                pl.semaphore_wait(relay.at[2], 2)
+                signal(relay.at[3], (g + 16 - 32 * xl, m))
+            if (h, k) == (1, 2):
+                pl.semaphore_wait(relay.at[3], 1)
+                give_weights()
 
     def sample(chunk):
         row = jnp.concatenate([cells[0, pl.ds(2 * chunk + i, 1), :] for i in range(2)], axis=1) // NC
@@ -359,32 +386,20 @@
             total = total + jnp.where(row == r, wide[r * 32:(r + 1) * 32], 0.0)
         return total.astype(BF16)
 
-    def scatter(d, carry):
-        peer = (m + d) % 16
-        sbuf[d] = sample(peer)
-        remote(sbuf.at[d], samples.at[m], s_s.at[d], r_s.at[m], (g, peer)).start()
-        return carry
-
-    lax.fori_loop(1, 16, scatter, 0)
+    def scatter(e, carry):
+        k = (e // 2) % 4
+        step = jnp.where(k < 2, 2 + k, 3 - k)
+        peer = ((m // 8 + 1 - e // 8) % 2) * 8 + ((m // 2 + step) % 4) * 2 + (m + 1 + e) % 2
+        sbuf[peer] = sample(peer)
+        remote(sbuf.at[peer], samples.at[m], s_s.at[peer], r_s.at[m], (g, peer)).start()
+        return carry
+
+    lax.fori_loop(0, 15, scatter, 0)
     samples[m] = sample(m)
-
-    pl.semaphore_wait(relay.at[2], 2)
-    signal(relay.at[3], (g + 16 - 32 * xl, m))
-    pl.semaphore_wait(relay.at[3], 1)
-
-    @pl.when(sender)
-    def _():
-        def give(d, carry):
-            s = (g + d) % 32
-            remote(wv.at[s], wrecv.at[g % 2], s_w.at[d], r_w.at[g % 2], (s, m)).start()
-            return carry
-
-        lax.fori_loop(1, 32, give, 0)
-        wrecv[g % 2] = wv[g]
 
     def scattered(d, carry):
         peer = (m + d) % 16
-        c = remote(sbuf.at[d], samples.at[peer], s_s.at[d], r_s.at[peer], (g, peer))
+        c = remote(sbuf.at[peer], samples.at[peer], s_s.at[peer], r_s.at[peer], (g, peer))
         c.wait_send()
         c.wait_recv()
         return carry
@@ -465,6 +480,7 @@
         return carry
 
     lax.fori_loop(0, 32, finish, 0)
+    stores[0].start()
 
     def plane_take(d, total):
         q = (p + d) % 16
@@ -473,6 +489,14 @@
 
     zsend[...] = lax.fori_loop(1, 16, plane_take, rcore[p])
 
+    def field_give(d, carry):
+        q = (m + d) % 16
+        mine = pbf.at[pl.ds(pl.multiple_of(q * 32, 32), 32)]
+        remote(mine, fields.at[m], s_f.at[d], r_f.at[m], (g, q)).start()
+        return carry
+
+    lax.fori_loop(1, 16, field_give, 0)
+    fields[m] = pbf[pl.ds(pl.multiple_of(m * 32, 32), 32), :]
     for j in range(6):
         @pl.when(z != z_reducer(j))
         def _(j=j):
@@ -507,50 +531,36 @@
 
     lax.fori_loop(1, 16, plane_send, 0)
 
+    def home(q):
+        return remote(fin.at[q], ff.at[core, q], s_b.at[q], r_b.at[q], (g, other))
+
+    home(p).start()
+    ff[core, p] = fin[p]
+
     def plane_got(d, carry):
         q = (p + d) % 16
         remote(fin.at[q], fin.at[q], s_a.at[d], r_a.at[q], plane_peer(q, g, m)).wait_recv()
+        home(q).start()
+        ff[core, q] = fin[q]
         return carry
 
     lax.fori_loop(1, 16, plane_got, 0)
-    home = remote(fin, ff.at[core], s_b.at[0], r_b.at[0], (g, other))
-    home.start()
-
-    def keep(i, carry):
-        ff[core, i] = fin[i]
-        return carry
-
-    lax.fori_loop(0, 16, keep, 0)
-    home.wait()
-
-    def field_give(d, carry):
-        q = (m + d) % 16
-        mine = pbf.at[pl.ds(pl.multiple_of(q * 32, 32), 32)]
-        remote(mine, fields.at[m], s_f.at[d], r_f.at[m], (g, q)).start()
-        return carry
-
-    lax.fori_loop(1, 16, field_give, 0)
-    fields[m] = pbf[pl.ds(pl.multiple_of(m * 32, 32), 32), :]
-    for i in range(2):
-        lanes = slice(i * 128, (i + 1) * 128)
-
-        @pl.when(2 * m + i != g)
-        def _(i=i, lanes=lanes):
-            src = samples.at[:, :, lanes]
-            remote(src, tall.at[g % 2], s_o.at[i], r_o.at[g % 2], (2 * m + i, g // 2)).start()
-
-        @pl.when(2 * m + i == g)
-        def _(i=i, lanes=lanes):
-            tall[g % 2] = samples[:, :, lanes]
-
-    solve(ff, asc, wsc, xcol)
+
+    def homed(q, carry):
+        home(q).wait_send()
+        remote(fin.at[q], ff.at[1 - core, q], s_b.at[q], r_b.at[q], (g, other)).wait_recv()
+        return carry
+
+    lax.fori_loop(0, 16, homed, 0)
+
+    solve(ff, asc, wsc, inv, xcol)
 
     x = xcol[...]
     shift = 1.0 / MEMBERS - jnp.sum(x[:, 0:1], axis=0, keepdims=True) / MEMBERS
     coefs = []
     for k in range(4):
         piece = x[k * 128:(k + 1) * 128].T[0:8, :]
-        mix_out[:, k * 128:(k + 1) * 128] = piece
+        mix_out[:, k * 128:(k + 1) * 128] = piece[0:1]
         coefs.append(piece + shift)
     pieces = split3(jnp.concatenate(coefs, axis=1))
 
@@ -559,6 +569,25 @@
         for piece in pieces:
             total = total + jnp.dot(piece, array, preferred_element_type=F32)
         return total[0:1]
+
+    slots = weigh(samples[...].reshape(MEMBERS, 256))
+    osend[0] = slots[:, 0:128]
+    osend[1] = slots[:, 128:256]
+
+    def show(d, carry):
+        o = 2 * m + d // 16
+        q = d % 16
+
+        @pl.when(jnp.logical_or(o != g, q != m))
+        def _():
+            remote(osend.at[d // 16], orecv.at[g], s_o.at[d], r_o.at[g], (o, q)).start()
+
+        @pl.when(jnp.logical_and(o == g, q == m))
+        def _():
+            orecv[g] = osend[d // 16]
+        return carry
+
+    lax.fori_loop(0, 32, show, 0)
 
     def field_take(d, carry):
         q = (m + d) % 16
@@ -569,16 +598,7 @@
         return carry
 
     lax.fori_loop(1, 16, field_take, 0)
-    for i in range(2):
-        @pl.when(2 * m + i != g)
-        def _(i=i):
-            src = samples.at[:, :, slice(0, 128)]
-            remote(src, tall.at[i], s_o.at[i], r_o.at[i], (2 * m + i, g // 2)).wait_recv()
-            remote(src, tall.at[i], s_o.at[i], r_o.at[i], (2 * m + i, g // 2)).wait_send()
-
-    parts = [weigh(fields[...].reshape(MEMBERS, NC))]
-    parts += [weigh(tall[i].reshape(MEMBERS, 128)) for i in range(2)]
-    line[m] = jnp.concatenate(parts, axis=1)
+    line[m] = weigh(fields[...].reshape(MEMBERS, NC))
 
     def line_give(d, carry):
         q = (m + d) % 16
@@ -617,20 +637,42 @@
 
     lax.fori_loop(1, 16, line_take, 0)
 
-    rows = jnp.concatenate([line[r][:, 0:NC] for r in range(16)], axis=0)
+    rows = jnp.concatenate([line[r] for r in range(16)], axis=0)
     total = jnp.zeros((16, NC), F32)
     for piece in split3(rows):
         total = total + lax.dot_general(piece, perm[...], (((1,), (1,)), ((), ())), preferred_element_type=F32)
     mean_out[...] = total
+
+    def seen(s, carry):
+        @pl.when(jnp.logical_or(s != g, m != g // 2))
+        def _():
+            remote(osend.at[0], orecv.at[s], s_o.at[0], r_o.at[s], (s, g // 2)).wait_recv()
+        return carry
+
+    lax.fori_loop(0, 32, seen, 0)
     for s in range(32):
-        first = NC + (s % 2) * 128
-        obs_out[s:s + 1, :] = line[s // 2][:, first:first + 128]
+        obs_out[s:s + 1, :] = orecv[s]
+    for store in stores[1:]:
+        store.start()
+
+    def shown(d, carry):
+        o = 2 * m + d // 16
+        q = d % 16
+
+        @pl.when(jnp.logical_or(o != g, q != m))
+        def _():
+            remote(osend.at[d // 16], orecv.at[g], s_o.at[d], r_o.at[g], (o, q)).wait_send()
+        return carry
+
+    lax.fori_loop(0, 32, shown, 0)
+    for store in stores:
+        store.wait()
 
 
 def local(
     prior_sample_matrix, cell_class, diffusion_table, velocity_table, obs_cells, obs_count, obs_value, obs_scale
 ):
-    vmem = pl.BlockSpec(memory_space=pltpu.VMEM)
+    hbm = pl.BlockSpec(memory_space=pl.ANY)
     smem = pl.BlockSpec(memory_space=pltpu.SMEM)
     dma = pltpu.SemaphoreType.DMA
     pred, mean, obs, mix = pl.pallas_call(
@@ -639,11 +681,22 @@
             jax.ShapeDtypeStruct((32, 16, NC), BF16),
             jax.ShapeDtypeStruct((16, NC), F32),
             jax.ShapeDtypeStruct((32, 128), F32),
-            jax.ShapeDtypeStruct((8, MEMBERS), F32),
+            jax.ShapeDtypeStruct((1, MEMBERS), F32),
         ),
-        in_specs=[vmem, vmem, smem, smem, vmem, smem, vmem, vmem],
-        out_specs=(vmem, vmem, vmem, vmem),
+        in_specs=[hbm, hbm, smem, smem, hbm, smem, hbm, hbm],
+        out_specs=(hbm, hbm, hbm, hbm),
         scratch_shapes=[
+            pltpu.VMEM((32, 16, NC), BF16),
+            pltpu.VMEM((16, NC), jnp.int32),
+            pltpu.VMEM((1, 32, 128), jnp.int32),
+            pltpu.VMEM((1, 32, 128), F32),
+            pltpu.VMEM((1, 32, 128), F32),
+            pltpu.VMEM((32, 16, NC), BF16),
+            pltpu.VMEM((16, NC), F32),
+            pltpu.VMEM((32, 128), F32),
+            pltpu.VMEM((1, MEMBERS), F32),
+            dma((5,)),
+            dma((4,)),
             pltpu.VMEM((8, 512, 128), F32),
             pltpu.VMEM((4, EXT, 8, NC), F32),
             pltpu.VMEM((4, EXT, 8, NC), F32),
@@ -668,21 +721,23 @@
             pltpu.VMEM((2, 16, 6, 8, 128), F32),
             pltpu.VMEM((4, 128, 640), F32),
             pltpu.VMEM((4, 128, 640), F32),
+            pltpu.VMEM((128, 128), F32),
             pltpu.VMEM((MEMBERS, 128), F32),
             pltpu.VMEM((16, 32, NC), BF16),
-            pltpu.VMEM((2, 16, 32, 128), BF16),
-            pltpu.VMEM((16, 1, NC + 256), F32),
+            pltpu.VMEM((2, 1, 128), F32),
+            pltpu.VMEM((32, 1, 128), F32),
+            pltpu.VMEM((16, 1, NC), F32),
             dma((2, 2)), dma((2, 2)), dma((2,)), dma((2,)), dma((32,)), dma((2,)), dma((16,)), dma((16,)),
             dma((1,)), dma((1,)), dma((16,)), dma((16,)), dma((6,)), dma((16,)), dma((16,)), dma((6,)),
-            dma((16,)), dma((16,)), dma((1,)), dma((1,)),
-            dma((16,)), dma((16,)), dma((2,)), dma((2,)), dma((16,)), dma((16,)),
+            dma((16,)), dma((16,)), dma((16,)), dma((16,)),
+            dma((16,)), dma((16,)), dma((32,)), dma((32,)), dma((16,)), dma((16,)),
             pltpu.SemaphoreType.REGULAR((4,)),
         ],
         compiler_params=pltpu.CompilerParams(
             collective_id=0, has_side_effects=True, vmem_limit_bytes=VMEM_LIMIT
         ),
     )(prior_sample_matrix, cell_class, diffusion_table, velocity_table, obs_cells, obs_count, obs_value, obs_scale)
-    return pred, mean, obs.reshape(1, 32, 128), mix[0]
+    return pred, mean, obs.reshape(1, 32, 128), mix.reshape(MEMBERS)
 
 
 def solution(mesh):

time: 137 us -> 113 us (0.82)
  Pallas kernels: 130 us -> 108 us
    pallas_call x1, Pallas kernels: 130 us -> 108 us  [local(): pl.pallas_call(kernel, out_shape=(jax.ShapeDtypeStruct((32, 16, NC), BF16...]
    unnamed x7 -> x10, local copies, waits for them, and re-layouts: 3.66 us -> 4.29 us
where the time goes in v3:
time: 113 us
  Pallas kernels  108 us (96%)
  local copies, waits for them, and re-layouts  4.29 us (4%)
    pallas_call x1, Pallas kernels, local(): pl.pallas_call(kernel, out_shape=(jax.ShapeDtypeStruct((32, 16, NC), BF16...  108 us
    unnamed x10, local copies, waits for them, and re-layouts  4.29 us

profile of v3, /device:TPU:1, one launch (start us, length us, event | category | flops | bytes accessed | tf_op | source)
XLA Modules:
  0.0 113.2 jit_solution(13754003871455974866)
XLA Ops:
  0.6 108.3 %shard_map.111 = (bf16[32,16,1024]{2,1,0:T(8,128)(2,1)}, f32[16,1024]{1,0:T(8,128)}, f32[32,128]{1,0:T(8,128)}, f32[1,512]{1,0:T(1,128)}) custom-call(bf16[32,16,1024]{2,1,0:T(8,128)(2,1)} %x_hbm.1, s32[16,1024]{1,0:T(8,128)} %cc_hbm.1, f32[16]{0:T(128)} %dif.1, f32[2,16]{1,0:T(2,128)} %vel.1, s32[1,32,128]{2,1,0:T(8,128)} %cells_hbm.1, s32[1,32]{1,0:T(1,128)} %count.1, ...), custom_call_target="tpu_custom_call" | custom-call | tf_op jit(solution)/shard_map/pallas_call | solution.py:678
  108.9 0.0 copy-start
  108.9 2.3 %copy.16 = bf16[32,16,1024]{2,1,0:T(8,128)(2,1)} copy(bf16[32,16,1024]{2,1,0:T(8,128)(2,1)} %get-tuple-element.16) | data formatting | bytes 2097152
  111.3 0.0 copy-done
  111.3 0.0 copy-start.1
  111.3 0.6 copy.17
  111.9 0.1 copy-done.1
  112.0 0.0 copy-start.2
  112.0 0.6 copy.18
  112.6 0.0 copy-done.2
  112.7 0.6 copy.19
Async XLA Ops:
  108.9 2.3 %copy-start = (f32[16,1024]{1,0:T(8,128)S(1)}, f32[16,1024]{1,0:T(8,128)}, u32[]{:S(2)}) copy-start(f32[16,1024]{1,0:T(8,128)} %get-tuple-element.17) | copy-start | bytes 196612
  111.3 0.7 copy-start.1
  112.0 0.7 copy-start.2

commit v4 on v3

--- a/solution.py
+++ b/solution.py
@@ -59,9 +59,9 @@
     return (value % 8) * 128 + value // 8
 
 
-def fill_coefs(g, cce, dif, vel, coef):
+def fill_coefs(quarters, g, cce, dif, vel, coef):
     place_of = lax.broadcasted_iota(jnp.int32, (8, NC), 1)
-    for quarter in range(4):
+    for quarter in quarters:
         rows = pl.ds(quarter * 8, 8)
         cls = cce[rows, :]
         d = jnp.zeros((8, NC), F32)
@@ -170,10 +170,10 @@
 def kernel(
     x_hbm, cc_hbm, dif, vel, cells_hbm, count, value_hbm, scale_hbm, pred_hbm, mean_hbm, obs_hbm, mix_hbm,
     x_ref, cc_ref, cells, value_ref, scale_ref, pred, mean_out, obs_out, mix_out, s_in, s_out,
-    turn, a_buf, b_buf, coef, perm, onehot, pbf, clsf, cce, hsend, hrecv, wv, wrecv, sbuf, samples,
-    fpart, rcore, rplane, zsend, zrecv, fin, ff, asc, wsc, inv, xcol, fields, osend, orecv, line,
+    turn, a_buf, b_buf, coef, perm, pbf, clsf, cce, hsend, hrecv, wv, wrecv, sbuf, samples,
+    fpart, rcore, rplane, zsend, zrecv, fin, ff, asc, wsc, inv, xcol, rows, fields, owned, opart, line,
     s_halo, r_halo, s_cls, r_cls, s_w, r_w, s_s, r_s, s_c, r_c, s_p, r_p, s_z, r_z, s_g, r_g, s_a, r_a, s_b, r_b,
-    s_f, r_f, s_o, r_o, s_l, r_l, relay,
+    s_f, r_f, s_o, r_o, s_l, r_l, s_q, r_q, relay,
 ):
     g, m = place()
     z, xl = g % 16, g // 16
@@ -263,6 +263,7 @@
 
     tell(0)
     cce[pl.ds(8, 16), :] = clsf[...]
+    fill_coefs((1, 2), g, cce, dif, vel, coef)
 
     @pl.when(g == 0)
     def _():
@@ -273,6 +274,59 @@
     def _():
         hrecv[1] = jnp.zeros((2, HALO, 16, NC), BF16)
         cce[pl.ds(24, 8), :] = jnp.zeros((8, NC), F32)
+
+    bufs = (a_buf, b_buf)
+
+    def edge(src, q, r):
+        return pltpu.roll(src[q, r, :, 7 * 128:], 1, 1), pltpu.roll(src[q, r, :, :128], 127, 1)
+
+    def advance(k, r, members):
+        src, dst = bufs[k % 2], bufs[(k + 1) % 2]
+        done = []
+        for q in members:
+            mid = [src[q, r, :, t * 128:(t + 1) * 128] for t in range(8)]
+            first, last = edge(src, q, r)
+            tiles = []
+            for t in range(8):
+                lanes = slice(t * 128, (t + 1) * 128)
+                c = [jnp.broadcast_to(coef[t, r + 2, i:i + 1, :], (8, 128)) for i in range(5)]
+                left = mid[t - 1] if t else first
+                right = mid[t + 1] if t < 7 else last
+                out = c[0] * mid[t]
+                out = out + c[1] * src[q, r - 1, :, lanes] + c[2] * src[q, r + 1, :, lanes]
+                out = out + c[3] * left + c[4] * right
+                if k < STEPS - 1:
+                    dst[q, r, :, lanes] = out
+                tiles.append(out)
+            done.append(jnp.concatenate(tiles, axis=1))
+        if k == STEPS - 1:
+            for h in range(len(members) // 2):
+                pair = jnp.concatenate(done[2 * h:2 * h + 2], axis=0).astype(BF16)
+                pbf[members[2 * h] // 2, r - HALO] = pair
+
+    pl.semaphore_wait(relay.at[0], 2)
+    tell(1)
+
+    for k in range(STEPS):
+        def inner(r, carry, k=k):
+            advance(k, r, (0, 1, 2, 3))
+            return carry
+
+        lax.fori_loop(HALO + 1 + k, EXT - HALO - 1 - k, inner, 0, unroll=2)
+        if k == 1:
+            pl.semaphore_wait(relay.at[1], 2)
+            tell(2)
+
+            @pl.when(g > 0)
+            def _():
+                up(1).start()
+
+            @pl.when(g < 31)
+            def _():
+                down(1).start()
+
+    pl.semaphore_wait(relay.at[2], 2)
+    signal(relay.at[3], (g + 16 - 32 * xl, m))
 
     for load in loads[2:]:
         load.wait()
@@ -280,35 +334,6 @@
     for s in range(32):
         valid = (slot < count[0, s]).astype(F32)
         wv[s] = jnp.concatenate([scale_ref[0, s:s + 1, :] * valid, value_ref[0, s:s + 1, :]], axis=1)
-    at_place = lax.broadcasted_iota(jnp.int32, (NC, 128), 0)
-
-    def mark(o, carry):
-        spot = across(cells[0, pl.ds(o, 1), :] % NC)
-        onehot[o] = (at_place == spot).astype(F32).astype(BF16)
-        return carry
-
-    lax.fori_loop(0, 32, mark, 0)
-
-    @pl.when(g > 0)
-    def _():
-        up(1).start()
-        cup.wait_send()
-        cdown.wait_recv()
-
-    @pl.when(g < 31)
-    def _():
-        down(1).start()
-        cdown.wait_send()
-        cup.wait_recv()
-
-    pl.semaphore_wait(relay.at[0], 2)
-    tell(1)
-
-    fill_coefs(g, cce, dif, vel, coef)
-    bufs = (a_buf, b_buf)
-
-    def edge(src, q, r):
-        return pltpu.roll(src[q, r, :, 7 * 128:], 1, 1), pltpu.roll(src[q, r, :, :128], 127, 1)
 
     def give_weights():
         @pl.when(sender)
@@ -321,6 +346,40 @@
             lax.fori_loop(1, 32, give, 0)
             wrecv[g % 2] = wv[g]
 
+    pl.semaphore_wait(relay.at[3], 1)
+    give_weights()
+
+    @pl.when(g > 0)
+    def _():
+        cup.wait_send()
+        cdown.wait_recv()
+
+    @pl.when(g < 31)
+    def _():
+        cdown.wait_send()
+        cup.wait_recv()
+
+    fill_coefs((0, 3), g, cce, dif, vel, coef)
+
+    at_place = lax.broadcasted_iota(jnp.int32, (256, 256), 0)
+
+    def sample(chunk):
+        cell = jnp.concatenate([cells[0, pl.ds(2 * chunk + i, 1), :] for i in range(2)], axis=1)
+        spot = across(cell % NC)
+        key = (cell // NC) * 4 + spot // 256
+        onehot = (at_place == spot % 256).astype(F32).astype(BF16)
+        state = pbf[...].reshape(512, NC)
+        tall = jnp.concatenate([state[:, 256 * b:256 * b + 256] for b in range(4)], axis=0)
+        wide = jnp.dot(tall, onehot, preferred_element_type=F32)
+        total = [jnp.zeros((16, 256), F32), jnp.zeros((16, 256), F32)]
+        for r in range(16):
+            for b in range(4):
+                hit = key == r * 4 + b
+                for h in range(2):
+                    at = b * 512 + h * 256 + r * 16
+                    total[h] = total[h] + jnp.where(hit, wide[at:at + 16], 0.0)
+        sbuf[chunk] = jnp.concatenate(total, axis=0).astype(BF16)
+
     for h in range(2):
         @pl.when(g > 0)
         def _(h=h):
@@ -341,61 +400,24 @@
 
             lax.fori_loop(0, HALO, widen, 0)
         for k in range(STEPS):
-            src, dst = bufs[k % 2], bufs[(k + 1) % 2]
-
-            def advance(r, carry, src=src, dst=dst, k=k, h=h):
-                pair = []
-                for q in (2 * h, 2 * h + 1):
-                    mid = [src[q, r, :, t * 128:(t + 1) * 128] for t in range(8)]
-                    first, last = edge(src, q, r)
-                    tiles = []
-                    for t in range(8):
-                        lanes = slice(t * 128, (t + 1) * 128)
-                        c = [jnp.broadcast_to(coef[t, r + 2, i:i + 1, :], (8, 128)) for i in range(5)]
-                        left = mid[t - 1] if t else first
-                        right = mid[t + 1] if t < 7 else last
-                        out = c[0] * mid[t]
-                        out = out + c[1] * src[q, r - 1, :, lanes] + c[2] * src[q, r + 1, :, lanes]
-                        out = out + c[3] * left + c[4] * right
-                        if k < STEPS - 1:
-                            dst[q, r, :, lanes] = out
-                        tiles.append(out)
-                    pair.append(jnp.concatenate(tiles, axis=1))
-                if k == STEPS - 1:
-                    pbf[pl.ds((r - HALO) * 32 + 16 * h, 16), :] = jnp.concatenate(pair, axis=0).astype(BF16)
+            def outer_rows(i, carry, k=k, h=h):
+                advance(k, k + 1 + i, (2 * h, 2 * h + 1))
+                advance(k, EXT - 2 - k - i, (2 * h, 2 * h + 1))
                 return carry
 
-            lax.fori_loop(k + 1, EXT - 1 - k, advance, 0, unroll=4)
-            if (h, k) == (0, 0):
-                pl.semaphore_wait(relay.at[1], 2)
-                tell(2)
-            if (h, k) == (0, 4):
-                pl.semaphore_wait(relay.at[2], 2)
-                signal(relay.at[3], (g + 16 - 32 * xl, m))
-            if (h, k) == (1, 2):
-                pl.semaphore_wait(relay.at[3], 1)
-                give_weights()
-
-    def sample(chunk):
-        row = jnp.concatenate([cells[0, pl.ds(2 * chunk + i, 1), :] for i in range(2)], axis=1) // NC
-        wide = jnp.dot(
-            pbf[...], jnp.concatenate([onehot[2 * chunk], onehot[2 * chunk + 1]], axis=1), preferred_element_type=F32
-        )
-        total = jnp.zeros((32, 256), F32)
-        for r in range(16):
-            total = total + jnp.where(row == r, wide[r * 32:(r + 1) * 32], 0.0)
-        return total.astype(BF16)
+            lax.fori_loop(0, HALO, outer_rows, 0, unroll=2)
 
     def scatter(e, carry):
         k = (e // 2) % 4
         step = jnp.where(k < 2, 2 + k, 3 - k)
         peer = ((m // 8 + 1 - e // 8) % 2) * 8 + ((m // 2 + step) % 4) * 2 + (m + 1 + e) % 2
-        sbuf[peer] = sample(peer)
+        sample(peer)
         remote(sbuf.at[peer], samples.at[m], s_s.at[peer], r_s.at[m], (g, peer)).start()
         return carry
 
     lax.fori_loop(0, 15, scatter, 0)
-    samples[m] = sample(m)
+    sample(m)
+    samples[m] = sbuf[m]
 
     def scattered(d, carry):
         peer = (m + d) % 16
@@ -465,14 +487,17 @@
 
     lax.fori_loop(1, 16, plane_give, 0)
 
+    flat = pbf[...].reshape(512, NC)
     for t in range(8):
         back = lax.dot_general(
-            pbf[...], perm[t * 128:(t + 1) * 128, :], (((1,), (1,)), ((), ())), preferred_element_type=F32
+            flat, perm[t * 128:(t + 1) * 128, :], (((1,), (1,)), ((), ())), preferred_element_type=F32
         )
-        for r in range(16):
-            for q in range(4):
-                at = r * 32 + q * 8
-                turn[t, pl.ds(q * 128 + r, 8, stride=16), :] = back[at:at + 8]
+        rows[:, :, :, t * 128:(t + 1) * 128] = back.astype(BF16).reshape(2, 16, 16, 128)
+        for h in range(2):
+            for r in range(16):
+                for q in range(2):
+                    at = h * 256 + r * 16 + q * 8
+                    turn[t, pl.ds((2 * h + q) * 128 + r, 8, stride=16), :] = back[at:at + 8]
 
     def finish(i, carry):
         for t in range(8):
@@ -491,12 +516,11 @@
 
     def field_give(d, carry):
         q = (m + d) % 16
-        mine = pbf.at[pl.ds(pl.multiple_of(q * 32, 32), 32)]
-        remote(mine, fields.at[m], s_f.at[d], r_f.at[m], (g, q)).start()
+        remote(rows.at[:, q], fields.at[m], s_f.at[d], r_f.at[m], (g, q)).start()
         return carry
 
     lax.fori_loop(1, 16, field_give, 0)
-    fields[m] = pbf[pl.ds(pl.multiple_of(m * 32, 32), 32), :]
+    fields[m] = rows[:, m]
     for j in range(6):
         @pl.when(z != z_reducer(j))
         def _(j=j):
@@ -530,6 +554,15 @@
         return carry
 
     lax.fori_loop(1, 16, plane_send, 0)
+
+    def own_give(d, carry):
+        o = (g + d) % 32
+        lanes = pl.ds(pl.multiple_of((o % 2) * 128, 128), 128)
+        remote(sbuf.at[o // 2, :, lanes], owned.at[g], s_o.at[d], r_o.at[g], (o, m)).start()
+        return carry
+
+    lax.fori_loop(1, 32, own_give, 0)
+    owned[g] = sbuf[g // 2, :, pl.ds(pl.multiple_of((g % 2) * 128, 128), 128)]
 
     def home(q):
         return remote(fin.at[q], ff.at[core, q], s_b.at[q], r_b.at[q], (g, other))
@@ -570,29 +603,30 @@
             total = total + jnp.dot(piece, array, preferred_element_type=F32)
         return total[0:1]
 
-    slots = weigh(samples[...].reshape(MEMBERS, 256))
-    osend[0] = slots[:, 0:128]
-    osend[1] = slots[:, 128:256]
-
-    def show(d, carry):
-        o = 2 * m + d // 16
-        q = d % 16
-
-        @pl.when(jnp.logical_or(o != g, q != m))
-        def _():
-            remote(osend.at[d // 16], orecv.at[g], s_o.at[d], r_o.at[g], (o, q)).start()
-
-        @pl.when(jnp.logical_and(o == g, q == m))
-        def _():
-            orecv[g] = osend[d // 16]
-        return carry
-
-    lax.fori_loop(0, 32, show, 0)
+    mine = xcol[pl.ds(pl.multiple_of(m * 32, 32), 32), :] + shift
+
+    def own_take(d, carry):
+        o = (g + d) % 32
+        lanes = pl.ds(pl.multiple_of((o % 2) * 128, 128), 128)
+        c = remote(sbuf.at[o // 2, :, lanes], owned.at[o], s_o.at[d], r_o.at[o], (o, m))
+        c.wait_send()
+        c.wait_recv()
+        return carry
+
+    lax.fori_loop(1, 32, own_take, 0)
+    sums = [jnp.sum(mine * owned[s].astype(F32), axis=0, keepdims=True) for s in range(32)]
+    opart[m] = jnp.concatenate(sums, axis=0)
+
+    def part_give(d, carry):
+        q = (m + d) % 16
+        remote(opart.at[m], opart.at[m], s_q.at[d], r_q.at[m], (g, q)).start()
+        return carry
+
+    lax.fori_loop(1, 16, part_give, 0)
 
     def field_take(d, carry):
         q = (m + d) % 16
-        mine = pbf.at[pl.ds(pl.multiple_of(q * 32, 32), 32)]
-        c = remote(mine, fields.at[q], s_f.at[d], r_f.at[q], (g, q))
+        c = remote(rows.at[:, q], fields.at[q], s_f.at[d], r_f.at[q], (g, q))
         c.wait_send()
         c.wait_recv()
         return carry
@@ -637,34 +671,23 @@
 
     lax.fori_loop(1, 16, line_take, 0)
 
-    rows = jnp.concatenate([line[r] for r in range(16)], axis=0)
-    total = jnp.zeros((16, NC), F32)
-    for piece in split3(rows):
-        total = total + lax.dot_general(piece, perm[...], (((1,), (1,)), ((), ())), preferred_element_type=F32)
-    mean_out[...] = total
-
-    def seen(s, carry):
-        @pl.when(jnp.logical_or(s != g, m != g // 2))
-        def _():
-            remote(osend.at[0], orecv.at[s], s_o.at[0], r_o.at[s], (s, g // 2)).wait_recv()
-        return carry
-
-    lax.fori_loop(0, 32, seen, 0)
-    for s in range(32):
-        obs_out[s:s + 1, :] = orecv[s]
+    mean_out[...] = jnp.concatenate([line[r] for r in range(16)], axis=0)
+
+    def part_take(d, carry):
+        q = (m + d) % 16
+        c = remote(opart.at[m], opart.at[q], s_q.at[d], r_q.at[q], (g, q))
+        c.wait_send()
+        c.wait_recv()
+        return carry
+
+    lax.fori_loop(1, 16, part_take, 0)
+    total = opart[0]
+    for q in range(1, 16):
+        total = total + opart[q]
+    obs_out[...] = total
     for store in stores[1:]:
         store.start()
 
-    def shown(d, carry):
-        o = 2 * m + d // 16
-        q = d % 16
-
-        @pl.when(jnp.logical_or(o != g, q != m))
-        def _():
-            remote(osend.at[d // 16], orecv.at[g], s_o.at[d], r_o.at[g], (o, q)).wait_send()
-        return carry
-
-    lax.fori_loop(0, 32, shown, 0)
     for store in stores:
         store.wait()
 
@@ -702,8 +725,7 @@
             pltpu.VMEM((4, EXT, 8, NC), F32),
             pltpu.VMEM((8, 32, 8, 128), F32),
             pltpu.VMEM((NC, NC), BF16),
-            pltpu.VMEM((32, NC, 128), BF16),
-            pltpu.VMEM((512, NC), BF16),
+            pltpu.VMEM((2, 16, 16, NC), BF16),
             pltpu.VMEM((16, NC), F32),
             pltpu.VMEM((32, NC), F32),
             pltpu.VMEM((2, 2, HALO, 16, NC), BF16),
@@ -723,14 +745,16 @@
             pltpu.VMEM((4, 128, 640), F32),
             pltpu.VMEM((128, 128), F32),
             pltpu.VMEM((MEMBERS, 128), F32),
-            pltpu.VMEM((16, 32, NC), BF16),
-            pltpu.VMEM((2, 1, 128), F32),
-            pltpu.VMEM((32, 1, 128), F32),
+            pltpu.VMEM((2, 16, 16, NC), BF16),
+            pltpu.VMEM((16, 2, 16, NC), BF16),
+            pltpu.VMEM((32, 32, 128), BF16),
+            pltpu.VMEM((16, 32, 128), F32),
             pltpu.VMEM((16, 1, NC), F32),
             dma((2, 2)), dma((2, 2)), dma((2,)), dma((2,)), dma((32,)), dma((2,)), dma((16,)), dma((16,)),
             dma((1,)), dma((1,)), dma((16,)), dma((16,)), dma((6,)), dma((16,)), dma((16,)), dma((6,)),
             dma((16,)), dma((16,)), dma((16,)), dma((16,)),
             dma((16,)), dma((16,)), dma((32,)), dma((32,)), dma((16,)), dma((16,)),
+            dma((16,)), dma((16,)),
             pltpu.SemaphoreType.REGULAR((4,)),
         ],
         compiler_params=pltpu.CompilerParams(

time: 113 us -> 111 us (0.982)
  Pallas kernels: 108 us -> 106 us
    pallas_call x1, Pallas kernels: 108 us -> 106 us  [local(): pl.pallas_call(kernel, out_shape=(jax.ShapeDtypeStruct((32, 16, NC), BF16...]
where the time goes in v4:
time: 111 us
  Pallas kernels  106 us (95%)
  local copies, waits for them, and re-layouts  4.29 us (4%)
    pallas_call x1, Pallas kernels, local(): pl.pallas_call(kernel, out_shape=(jax.ShapeDtypeStruct((32, 16, NC), BF16...  106 us
    unnamed x10, local copies, waits for them, and re-layouts  4.29 us

profile of v4, /device:TPU:1, one launch (start us, length us, event | category | flops | bytes accessed | tf_op | source)
XLA Modules:
  0.0 110.8 jit_solution(14902650286061952197)
XLA Ops:
  0.6 105.9 %shard_map.111 = (bf16[32,16,1024]{2,1,0:T(8,128)(2,1)}, f32[16,1024]{1,0:T(8,128)}, f32[32,128]{1,0:T(8,128)}, f32[1,512]{1,0:T(1,128)}) custom-call(bf16[32,16,1024]{2,1,0:T(8,128)(2,1)} %x_hbm.1, s32[16,1024]{1,0:T(8,128)} %cc_hbm.1, f32[16]{0:T(128)} %dif.1, f32[2,16]{1,0:T(2,128)} %vel.1, s32[1,32,128]{2,1,0:T(8,128)} %cells_hbm.1, s32[1,32]{1,0:T(1,128)} %count.1, ...), custom_call_target="tpu_custom_call" | custom-call | tf_op jit(solution)/shard_map/pallas_call | solution.py:701
  106.5 0.0 copy-start
  106.5 2.3 %copy.16 = bf16[32,16,1024]{2,1,0:T(8,128)(2,1)} copy(bf16[32,16,1024]{2,1,0:T(8,128)(2,1)} %get-tuple-element.16) | data formatting | bytes 2097152
  108.9 0.0 copy-done
  108.9 0.0 copy-start.1
  108.9 0.6 copy.17
  109.5 0.1 copy-done.1
  109.6 0.0 copy-start.2
  109.6 0.6 copy.18
  110.2 0.0 copy-done.2
  110.2 0.6 copy.19
Async XLA Ops:
  106.5 2.3 %copy-start = (f32[16,1024]{1,0:T(8,128)S(1)}, f32[16,1024]{1,0:T(8,128)}, u32[]{:S(2)}) copy-start(f32[16,1024]{1,0:T(8,128)} %get-tuple-element.17) | copy-start | bytes 196612
  108.9 0.7 copy-start.1
  109.6 0.7 copy-start.2
